TPU v7x, 128 devices: a whole 4x4x4 slice. The times are simulated.
128 devices in a mesh: lat: 8 (over x_hi, z), lon: 16 (over y, x_lo, core).
Axes of the slice: x: 4 (x_hi: 2, x_lo: 2; x = x_hi * 2 + x_lo), y: 4, z: 4, core: 2. Of those that a mesh axis runs over, the one named last changes fastest.
Arguments:
- level_one: bfloat16 [128, 512, 512], P('lat', 'lon'), may hold values from -6 to 6
- gain_attn: float32 [512], replicated, may hold values from 0.5 to 1.5
- w_qkv: bfloat16 [512, 1536], replicated, may hold values from -8 to 8
- w_proj: bfloat16 [512, 512], replicated, may hold values from -0.25 to 0.25
- gain_merge: float32 [2048], replicated, may hold values from 0.5 to 1.5
- w_merge: bfloat16 [2048, 1024], replicated, may hold values from -0.125 to 0.125
- gain_mlp: float32 [1024], replicated, may hold values from 0.5 to 1.5
- w_up: bfloat16 [1024, 4096], P(None, 'lon'), may hold values from -0.1875 to 0.1875
- w_down: bfloat16 [4096, 1024], P('lon'), may hold values from -0.09375 to 0.09375
- cotangent: bfloat16 [64, 256, 1024], P('lat', 'lon'), may hold values from -6 to 6
Outputs:
- level_two: bfloat16 [64, 256, 1024], P('lat', 'lon')
- grad_skip: bfloat16 [128, 512, 512], P('lat', 'lon')
- grad_proj: float32 [512, 512], replicated
- grad_merge: float32 [2048, 1024], P(('lat', 'lon'))
- grad_up: float32 [1024, 4096], P(None, 'lon')
- grad_down: float32 [4096, 1024], P('lon')
All inputs are finite; a program needn't handle non-finite values.
Results may differ from a plain program's by a relative error of at most 0.029.
Values may be sent and summed in bfloat16 or wider, within the bound.
No kernel may reach another device: no remote copies, remote signals or barrier semaphores. Data moves between devices by JAX's collectives and lax.ppermute only.
A program may use at most 128 MiB of HBM per device.

v0:
```python
import jax
import jax.numpy as jnp
from jax import lax
from jax.experimental import pallas as pl
from jax.experimental.pallas import tpu as pltpu
from jax.sharding import Mesh
from jax.sharding import PartitionSpec as P

HD = 64
WIN = 8
SHIFT = 4
LAT = ("xh", "z")
LON = ("y", "xl", "c")
F32 = jnp.float32
BF = jnp.bfloat16
VMEM = pl.BlockSpec(memory_space=pltpu.VMEM)
HBM = pl.BlockSpec(memory_space=pl.ANY)
SMEM = pl.BlockSpec(memory_space=pltpu.SMEM)


def rotate(value, axis, shift):
    size = lax.axis_size(axis)
    return lax.ppermute(value, axis, [(i, (i + shift) % size) for i in range(size)])


def params():
    return pltpu.CompilerParams(vmem_limit_bytes=62 * 2**20)


def cost():
    return pl.CostEstimate(flops=1000, bytes_accessed=1000, transcendentals=0)


def together(*values):
    return lax.optimization_barrier(values)


def scatter_rel(parts, axis, way):
    total = parts[0].astype(F32)
    for k in range(1, len(parts)):
        total = total + rotate(parts[k], axis, way * k).astype(F32)
    return total


def gather_rel(value, axis):
    return [value] + [rotate(value, axis, k) for k in range(1, lax.axis_size(axis))]


def normalise(values, gain):
    center = values - jnp.mean(values, axis=-1, keepdims=True)
    spread = jnp.mean(center * center, axis=-1, keepdims=True)
    return center * lax.rsqrt(spread + 1e-05) * gain


def nt(a, b):
    return lax.dot_general(a, b, (((1,), (1,)), ((), ())), preferred_element_type=F32)


def tn(a, b):
    return lax.dot_general(a, b, (((0,), (0,)), ((), ())), preferred_element_type=F32)


def attend_kernel(
    place_ref, own_ref, top_ref, bottom_ref, left_ref, right_ref, gain_attn_ref, qkv_ref, proj_ref,
    gain_merge_ref, merge_ref, gain_mlp_ref,
    norm_out, coarse_out, merged_out, pick_out, att_out,
    field, att, hold, proj_all, merge_all, proj_sem, merge_sem,
):
    proj_copy = pltpu.make_async_copy(proj_ref, proj_all, proj_sem)
    merge_copy = pltpu.make_async_copy(merge_ref, merge_all, merge_sem)
    proj_copy.start()
    merge_copy.start()
    rows, cols, width = own_ref.shape
    lanes = width // 128
    for n in range(lanes):
        part = slice(n * 128, (n + 1) * 128)
        field[n, SHIFT : SHIFT + rows, SHIFT : SHIFT + cols, :] = own_ref[:, :, part].astype(F32)
        field[n, :SHIFT, SHIFT : SHIFT + cols, :] = top_ref[:, :, part].astype(F32)
        field[n, SHIFT + rows :, SHIFT : SHIFT + cols, :] = bottom_ref[:, :, part].astype(F32)
        field[n, :, :SHIFT, :] = left_ref[:, :, part].astype(F32)
        field[n, :, SHIFT + cols :, :] = right_ref[:, :, part].astype(F32)
    across = (cols + WIN) // WIN
    size = WIN * WIN
    low = lax.broadcasted_iota(jnp.int32, (size, 128), 1) < HD
    key_row = lax.broadcasted_iota(jnp.int32, (2 * size, size), 1) // WIN
    first = place_ref[0] * rows - SHIFT
    total = place_ref[1] * rows

    def band(a, carry):
        for b in range(across):
            x = jnp.concatenate(
                [
                    field[n, pl.ds(a * WIN, WIN), b * WIN : (b + 1) * WIN, :].reshape(size, 128)
                    for n in range(lanes)
                ],
                axis=1,
            )
            hold[b * size : (b + 1) * size, :] = normalise(x, gain_attn_ref[...]).astype(BF)
        qkv = jnp.dot(hold[...], qkv_ref[...], preferred_element_type=F32).astype(BF)
        row = first + a * WIN + key_row
        allowed = (row >= 0) & (row < total)
        for b in range(across):
            here = slice(b * size, (b + 1) * size)
            for p in range(lanes):
                q = qkv[here, p * 128 : (p + 1) * 128]
                k = qkv[here, width + p * 128 : width + (p + 1) * 128]
                v = qkv[here, 2 * width + p * 128 : 2 * width + (p + 1) * 128]
                none = jnp.zeros_like(q)
                pair = jnp.concatenate([jnp.where(low, q, none), jnp.where(low, none, q)], axis=0)
                scores = jnp.where(allowed, nt(pair, k) * (1.0 / 8.0), -1e30)
                expo = jnp.exp(scores - jnp.max(scores, axis=1, keepdims=True))
                weights = (expo / jnp.sum(expo, axis=1, keepdims=True)).astype(BF)
                both = jnp.dot(weights, v, preferred_element_type=F32)
                out = jnp.where(low, both[:size], both[size:]).astype(BF).astype(F32)
                att[p, pl.ds(a * WIN, WIN), b * WIN : (b + 1) * WIN, :] = out.reshape(WIN, WIN, 128)
        return carry

    lax.fori_loop(0, (rows + WIN) // WIN, band, 0)

    proj_copy.wait()
    half_rows, half_cols = rows // 2, cols // 2
    tokens = half_rows * half_cols
    pieces = []
    for p in range(4):
        di, dj = p % 2, p // 2
        def pick(ref):
            return jnp.concatenate(
                [
                    jnp.concatenate(
                        [
                            ref[n, SHIFT + di + 2 * i, pl.ds(SHIFT + dj, half_cols, stride=2), :]
                            for i in range(half_rows)
                        ],
                        axis=0,
                    )
                    for n in range(lanes)
                ],
                axis=1,
            )
        got = pick(att).astype(BF)
        att_out[:, p * width : (p + 1) * width] = got
        block = pick(field) + jnp.dot(got, proj_all[...], preferred_element_type=F32)
        block = block.astype(BF)
        merged_out[:, p * width : (p + 1) * width] = block
    merged = merged_out[...].astype(F32)
    merged_norm = normalise(merged, gain_merge_ref[...]).astype(BF)
    for n in range(4):
        pick_out[n] = jnp.concatenate(
            [merged_norm[:, g * 256 + n * 64 : g * 256 + (n + 1) * 64] for g in range(8)], axis=1
        )
    merge_copy.wait()
    coarse = jnp.dot(merged_norm, merge_all[...], preferred_element_type=F32).astype(BF)
    coarse_out[...] = coarse
    norm_out[...] = normalise(coarse.astype(F32), gain_mlp_ref[...]).astype(BF)


def attend(place, own, top, bottom, left, right, gain_attn, w_qkv, w_proj, gain_merge, w_merge, gain_mlp):
    rows, cols, width = own.shape
    tokens = rows * cols // 4
    wide = w_merge.shape[1]
    shapes = [
        jax.ShapeDtypeStruct((tokens, wide), BF),
        jax.ShapeDtypeStruct((tokens, wide), BF),
        jax.ShapeDtypeStruct((tokens, 4 * width), BF),
        jax.ShapeDtypeStruct((4, tokens, width), BF),
        jax.ShapeDtypeStruct((tokens, 4 * width), BF),
    ]
    return pl.pallas_call(
        attend_kernel,
        out_shape=shapes,
        in_specs=[SMEM]
        + [VMEM] * 7
        + [HBM, VMEM, HBM, VMEM],
        out_specs=[VMEM] * 5,
        scratch_shapes=[
            pltpu.VMEM((width // 128, rows + WIN, cols + WIN, 128), F32),
            pltpu.VMEM((width // 128, rows + WIN, cols + WIN, 128), F32),
            pltpu.VMEM(((cols + WIN) * WIN, width), BF),
            pltpu.VMEM(w_proj.shape, BF),
            pltpu.VMEM(w_merge.shape, BF),
            pltpu.SemaphoreType.DMA,
            pltpu.SemaphoreType.DMA,
        ],
        compiler_params=params(),
        cost_estimate=cost(),
    )(place, own, top, bottom, left, right, gain_attn.reshape(1, -1), w_qkv, w_proj, gain_merge.reshape(1, -1), w_merge, gain_mlp.reshape(1, -1))


def hidden_kernel(*refs):
    norms, streams, ups, downs, parts = (refs[i : i + 4] for i in range(0, 20, 4))
    hidden_out, pre_out, norm_all, stream_all, total = refs[20:]
    tokens = norms[0].shape[0]
    chunk = ups[0].shape[1]
    for t in range(4):
        norm_all[t * tokens : (t + 1) * tokens, :] = norms[t][...]
        stream_all[t * tokens : (t + 1) * tokens, :] = streams[t][...]
    for m in range(4):
        up = ups[m][...]
        pre = jnp.dot(norm_all[...], up, preferred_element_type=F32)
        grad_hidden = nt(stream_all[...], downs[m][...])
        tangent = jnp.tanh(0.7978845608 * (pre + 0.044715 * pre * pre * pre))
        hidden = 0.5 * pre * (1.0 + tangent)
        slope = 0.5 * (1.0 + tangent) + 0.5 * pre * (1.0 - tangent * tangent) * 0.7978845608 * (
            1.0 + 3.0 * 0.044715 * pre * pre
        )
        here = slice(m * chunk, (m + 1) * chunk)
        hidden_out[:, here] = hidden.astype(BF)
        grad_pre = (grad_hidden * slope).astype(BF)
        pre_out[:, here] = grad_pre
        part = nt(grad_pre, up)
        if m == 0:
            total[...] = part
        elif m < 3:
            total[...] += part
        else:
            for t in range(4):
                rows = slice(t * tokens, (t + 1) * tokens)
                parts[t][...] = (total[rows, :] + part[rows, :]).astype(BF)


def hidden_units(norms, streams, ups, downs):
    tokens, width = norms[0].shape
    chunk = ups[0].shape[1]
    out = [jax.ShapeDtypeStruct((tokens, width), BF)] * 4
    out += [jax.ShapeDtypeStruct((4 * tokens, 4 * chunk), BF)] * 2
    return pl.pallas_call(
        hidden_kernel,
        out_shape=out,
        in_specs=[VMEM] * 16,
        out_specs=[VMEM] * 6,
        scratch_shapes=[
            pltpu.VMEM((4 * tokens, width), BF),
            pltpu.VMEM((4 * tokens, width), BF),
            pltpu.VMEM((4 * tokens, width), F32),
        ],
        compiler_params=params(),
        cost_estimate=cost(),
    )(*norms, *streams, *ups, *downs)


def weight_grad_kernel(*refs):
    place, norms, streams, hidden, pre = refs[0], refs[1:5], refs[5:9], refs[9], refs[10]
    send, keep, norm_all, stream_all = refs[11:]
    tokens = norms[0].shape[0]
    chunk = pre.shape[1] // 4
    for t in range(4):
        norm_all[t * tokens : (t + 1) * tokens, :] = norms[t][...]
        stream_all[t * tokens : (t + 1) * tokens, :] = streams[t][...]
    for m in (1, 3, 0, 2):
        here = slice(m * chunk, (m + 1) * chunk)
        up = tn(norm_all[...], pre[:, here]).astype(BF)
        down = tn(hidden[:, here], stream_all[...]).astype(BF)
        target = send if m % 2 else keep
        side = lax.rem(place[4] + m // 2, 2)
        for n in range(8):
            block = slice(n * 128, (n + 1) * 128)
            target[n * 2 + side, :128, :] = up[block, :]
            target[n * 2 + side, 128:, :128] = down[:128, block]
            target[n * 2 + side, 128:, 128:] = down[128:, block]


def weight_grads(place, norms, streams, hidden, pre):
    tokens, width = norms[0].shape
    return pl.pallas_call(
        weight_grad_kernel,
        out_shape=[jax.ShapeDtypeStruct((16, 256, 256), BF)] * 2,
        in_specs=[SMEM] + [VMEM] * 10,
        out_specs=[VMEM] * 2,
        scratch_shapes=[pltpu.VMEM((4 * tokens, width), BF), pltpu.VMEM((4 * tokens, width), BF)],
        compiler_params=params(),
        cost_estimate=cost(),
    )(place, *norms, *streams, hidden, pre)


def add(a, b):
    return (a.astype(F32) + b.astype(F32)).astype(BF)


def pair_sum_kernel(keep, got, out):
    out[...] = add(keep[...], got[...])


def all_sum_kernel(blocks, merges, out, merge_out):
    total = blocks[0].astype(F32)
    merge = merges[0].astype(F32)
    for n in range(1, blocks.shape[0]):
        total += blocks[n].astype(F32)
        merge += merges[n].astype(F32)
    for n in range(4):
        merge_out[:, n * 256 : (n + 1) * 256] = merge[n * 16 : (n + 1) * 16, :]
    total = total.astype(BF)
    proj = merge[64:, :].astype(BF)
    for n in range(out.shape[0]):
        out[n, :256, :] = total
        out[n, 256:, :] = proj


def merge_pack_kernel(merge_keep, merge_got, proj_keep, proj_got, out):
    for p in range(out.shape[0]):
        merge = add(merge_keep[p], merge_got[p])
        for n in range(4):
            out[p, n * 16 : (n + 1) * 16, :] = merge[:, n * 256 : (n + 1) * 256]
        out[p, 64:, :] = add(proj_keep[p // 2], proj_got[p // 2])


def sums(kernel, shapes, *args):
    return pl.pallas_call(
        kernel,
        out_shape=[
            jax.ShapeDtypeStruct(shape, F32 if shape == (16, 1024) else BF) for shape in shapes
        ],
        in_specs=[VMEM] * len(args),
        out_specs=[VMEM] * len(shapes),
        compiler_params=params(),
        cost_estimate=cost(),
    )(*args)


def down_kernel(*refs):
    hidden, downs, parts = refs[0], refs[1:5], refs[5:]
    tokens = parts[0].shape[0]
    chunk = downs[0].shape[0]
    for t in range(4):
        rows = slice(t * tokens, (t + 1) * tokens)
        total = 0.0
        for m in range(4):
            total += jnp.dot(
                hidden[rows, m * chunk : (m + 1) * chunk],
                downs[m][...],
                preferred_element_type=F32,
            )
        parts[t][...] = total.astype(BF)


def down_parts(hidden, downs):
    tokens = hidden.shape[0] // 4
    return pl.pallas_call(
        down_kernel,
        out_shape=[jax.ShapeDtypeStruct((tokens, downs[0].shape[1]), BF)] * 4,
        in_specs=[VMEM] * 5,
        out_specs=[VMEM] * 4,
        compiler_params=params(),
        cost_estimate=cost(),
    )(hidden, *downs)


def merge_grad_kernel(place, left, right0, right1, right2, right3, keep, send, both, left_all, right_all):
    tokens, width = left.shape[1:]
    for t, right in enumerate((right0, right1, right2, right3)):
        left_all[t * tokens : (t + 1) * tokens, :] = left[lax.rem(place[2] + 4 - t, 4)]
        right_all[t * tokens : (t + 1) * tokens, :] = right[...]
    part = tn(left_all[...], right_all[...]).astype(BF)
    for n in range(width // 16):
        both[lax.rem(n % 2 + place[5], 2), n // 2] = part[n * 16 : (n + 1) * 16, :]
    keep[...] = both[0]
    send[...] = both[1]


def merge_grads(place, left, rights):
    tokens, width = left.shape[1:]
    last = rights[0].shape[-1]
    return pl.pallas_call(
        merge_grad_kernel,
        out_shape=[jax.ShapeDtypeStruct((width // 32, 16, last), BF)] * 2,
        in_specs=[SMEM] + [VMEM] * 5,
        out_specs=[VMEM] * 2,
        scratch_shapes=[
            pltpu.VMEM((2, width // 32, 16, last), BF),
            pltpu.VMEM((4 * tokens, width), BF),
            pltpu.VMEM((4 * tokens, last), BF),
        ],
        compiler_params=params(),
        cost_estimate=cost(),
    )(place, left, *rights)


def place_kernel(blocks, up, down):
    for n in range(8):
        block = slice(n * 128, (n + 1) * 128)
        up[block, :] = blocks[n, :128, :].astype(F32)
        down[:128, block] = blocks[n, 128:256, :128].astype(F32)
        down[128:, block] = blocks[n, 128:256, 128:].astype(F32)


def place_blocks(blocks):
    return pl.pallas_call(
        place_kernel,
        out_shape=[
            jax.ShapeDtypeStruct((1024, 256), F32),
            jax.ShapeDtypeStruct((256, 1024), F32),
        ],
        in_specs=[VMEM],
        out_specs=[VMEM] * 2,
        compiler_params=params(),
        cost_estimate=cost(),
    )(blocks)


def proj_kernel(place, own, other, out):
    for k in range(4):
        y = lax.rem(place[2] + 4 - k, 4)
        for side, ref in enumerate((own, other)):
            c = lax.rem(place[5] + side, 2)
            for n in range(8):
                start = pl.multiple_of((y * 16 + c * 8 + n) * 8, 8)
                block = ref[k, n].astype(F32)
                out[pl.ds(start, 8), :256] = block[:8, :]
                out[pl.ds(start, 8), 256:] = block[8:, :]


def place_proj(place, own, other):
    return pl.pallas_call(
        proj_kernel,
        out_shape=jax.ShapeDtypeStruct((512, 512), F32),
        in_specs=[SMEM] + [VMEM] * 2,
        out_specs=VMEM,
        compiler_params=params(),
        cost_estimate=cost(),
    )(place, own, other)


def norm_back(values, gain, upstream):
    center = values - jnp.mean(values, axis=-1, keepdims=True)
    spread = jnp.mean(center * center, axis=-1, keepdims=True)
    factor = lax.rsqrt(spread + 1e-05)
    normal = center * factor
    scaled = upstream * gain
    return factor * (
        scaled
        - jnp.mean(scaled, axis=-1, keepdims=True)
        - normal * jnp.mean(scaled * normal, axis=-1, keepdims=True)
    )


def skip_kernel(
    place, coarse_grad, gain, merge, merged, att, skip, proj0, proj1, proj2, proj3, hold, blocks
):
    lanes = hold.shape[0]
    width = lanes * 128
    half_rows, half_cols = hold.shape[1] // 2, hold.shape[2] // 2
    grad = nt(coarse_grad[...], merge[...])
    grad = norm_back(merged[...].astype(F32), gain[...], grad).astype(BF)
    total = None
    for p in range(4):
        di, dj = p % 2, p // 2
        piece = grad[:, p * width : (p + 1) * width]
        part = tn(att[:, p * width : (p + 1) * width], piece)
        total = part if total is None else total + part
        wide = piece.astype(F32)
        for n in range(lanes):
            for i in range(half_rows):
                hold[n, di + 2 * i, pl.ds(dj, half_cols, stride=2), :] = wide[
                    i * half_cols : (i + 1) * half_cols, n * 128 : (n + 1) * 128
                ]
    for n in range(lanes):
        skip[:, :, n * 128 : (n + 1) * 128] = hold[n].astype(BF)
    for n in range(width // 8):
        dy = lax.rem(n // 16 + 4 - place[2], 4)
        dc = lax.rem(n // 8 % 2 + place[5], 2)
        rows = slice(n * 8, (n + 1) * 8)
        block = jnp.concatenate([total[rows, : width // 2], total[rows, width // 2 :]], axis=0)
        blocks[dy, dc, n % 8] = block.astype(BF)
    for n, out in enumerate((proj0, proj1, proj2, proj3)):
        out[...] = blocks[n]


def skip_grads(place, coarse_grad, gain, merge, merged, att, rows, cols):
    width = att.shape[1] // 4
    return pl.pallas_call(
        skip_kernel,
        out_shape=[
            jax.ShapeDtypeStruct((rows, cols, width), BF),
        ]
        + [jax.ShapeDtypeStruct((2, 8, 16, width // 2), BF)] * 4,
        in_specs=[SMEM] + [VMEM] * 5,
        out_specs=[VMEM] * 5,
        scratch_shapes=[
            pltpu.VMEM((width // 128, rows, cols, 128), F32),
            pltpu.VMEM((4, 2, 8, 16, width // 2), BF),
        ],
        compiler_params=params(),
        cost_estimate=cost(),
    )(place, coarse_grad, gain.reshape(1, -1), merge, merged, att)


def per_device(
    level_one, gain_attn, w_qkv, w_proj, gain_merge, w_merge, gain_mlp, w_up, w_down, cotangent
):
    tile_rows, tile_cols, feature = level_one.shape
    width = cotangent.shape[-1]
    upstream = cotangent.reshape(-1, width)
    place = jnp.stack(
        [lax.axis_index(LAT), jnp.int32(lax.axis_size(LAT))]
        + [lax.axis_index(name) for name in ("y", "z", "xl", "c", "xh")]
    ).astype(jnp.int32)

    top = rotate(level_one[-SHIFT:], LAT, 1)
    bottom = rotate(level_one[:SHIFT], LAT, -1)
    top, bottom = together(top, bottom)

    tall = [top, level_one, bottom]
    left = rotate(jnp.concatenate([part[:, -SHIFT:] for part in tall], axis=0), LON, 1)
    right = rotate(jnp.concatenate([part[:, :SHIFT] for part in tall], axis=0), LON, -1)
    left, right, first_up, first_down, upstream = together(
        left, right, w_up, w_down, upstream
    )

    coarse_norm, coarse, merged, picks, att = attend(
        place, level_one, top, bottom, left, right, gain_attn, w_qkv, w_proj,
        gain_merge, w_merge, gain_mlp,
    )
    up_x, up_c = rotate(first_up, "xl", 1), rotate(first_up, "c", 1)
    streams = gather_rel(upstream, "y")
    coarse_norm, picks, up_x, up_c, streams, first_down = together(
        coarse_norm, picks, up_x, up_c, streams, first_down
    )

    down_x, up_xc = rotate(first_down, "xl", 1), rotate(up_x, "c", 1)
    norms = gather_rel(coarse_norm, "y")
    norms, up_xc, down_x, picks, first_down = together(norms, up_xc, down_x, picks, first_down)

    down_c, down_xc = rotate(first_down, "c", 1), rotate(down_x, "c", 1)
    lefts = lax.all_to_all(picks, "y", 0, 0)
    ups, downs = [w_up, up_c, up_x, up_xc], [w_down, down_c, down_x, down_xc]
    *parts, hidden, grad_pre = hidden_units(norms, streams, ups, downs)
    parts, hidden, grad_pre, lefts = together(parts, hidden, grad_pre, lefts)

    arrived = [rotate(parts[k], "y", -k) for k in range(1, 4)]
    send, keep = weight_grads(place, norms, streams, hidden, grad_pre)
    (blocks,) = sums(pair_sum_kernel, [(16, 256, 256)], keep, rotate(send, "c", 1))
    outer = down_parts(hidden, downs)
    arrived, outer = together(arrived, outer)
    grad_norm = sum(part.astype(F32) for part in [parts[0]] + arrived)
    grad_coarse = (
        upstream.astype(F32) + norm_back(coarse.astype(F32), gain_mlp, grad_norm)
    ).astype(BF)

    blocks = lax.all_to_all(blocks, LAT + ("xl",), 0, 0)
    rights = gather_rel(grad_coarse, "y")
    grad_skip, *projs = skip_grads(
        place, grad_coarse, gain_merge, w_merge, merged, att, tile_rows, tile_cols
    )
    rights, grad_skip = together(rights, grad_skip)
    proj = sum(
        part.astype(F32)
        for part in [projs[0]] + [rotate(projs[k], "y", k) for k in range(1, 4)]
    ).astype(BF)
    proj_got = rotate(proj[1], "c", 1)
    merge_keep, merge_send = merge_grads(place, lefts, rights)
    merge_got = rotate(merge_send, "c", 1)
    (merges,) = sums(
        merge_pack_kernel, [(16, 80, 256)], merge_keep, merge_got, proj[0], proj_got
    )
    blocks, merges, outer = together(blocks, merges, outer)

    merges = lax.all_to_all(merges, LAT + ("xl",), 0, 0)
    merges, outer = together(merges, outer)

    blocks, grad_merge = sums(all_sum_kernel, [(8, 272, 256), (16, 1024)], blocks, merges)
    blocks = lax.all_to_all(blocks, LAT, 0, 0)
    summed = scatter_rel(outer, "y", -1)
    level_two = (coarse.astype(F32) + summed).astype(BF)
    blocks, level_two = together(blocks, level_two)

    proj = jnp.stack(gather_rel(blocks[:, 256:], "y"))
    grad_up, grad_down = place_blocks(blocks)
    grad_proj = place_proj(place, proj, rotate(proj, "c", 1))

    level_two = level_two.reshape(tile_rows // 2, tile_cols // 2, width)
    return (level_two, grad_skip, grad_proj, grad_merge, grad_up, grad_down)


def solution(mesh):
    fine = Mesh(mesh.devices.reshape(2, 4, 4, 2, 2), LAT + LON)
    grid = P(LAT, LON, None)
    placed = (grid, P(), P(), P(), P(), P(), P(), P(None, LON), P(LON, None), grid)
    return jax.shard_map(
        per_device,
        mesh=fine,
        in_specs=placed,
        out_specs=(grid, grid, P(), P(LAT + LON, None), P(None, LON), P(LON, None)),
        check_vma=False,
    )
```

profile of v0, /device:TPU:1, one launch (start us, length us, event | category | flops | bytes accessed | tf_op | source)
XLA Modules:
  0.0 182.3 jit_solution(7144506459180154080)
XLA Ops:
  0.6 1.0 fusion.13
  1.6 2.5 %collective-permute-start = (bf16[4,32,512]{2,1,0:T(8,128)(2,1)S(1)}, bf16[4,32,512]{2,1,0:T(8,128)(2,1)S(1)}, u32[]{:S(2)}, u32[]{:S(2)}) collective-permute-start(bf16[4,32,512]{2,1,0:T(8,128)(2,1)S(1)} %get-tuple-element.182), channel_id=1, source_target_pairs={{0,16},{16,32},{32,48},{48,64},{64,80},{80,96},{96,112},{112,0},{1... | collective-permute-start | bytes 393224 | tf_op jit(solution)/shard_map/ppermute | solution.py:23
  4.2 4.7 %collective-permute-start.1 = (bf16[4,32,512]{2,1,0:T(8,128)(2,1)S(1)}, bf16[4,32,512]{2,1,0:T(8,128)(2,1)S(1)}, u32[]{:S(2)}, u32[]{:S(2)}) collective-permute-start(bf16[4,32,512]{2,1,0:T(8,128)(2,1)S(1)} %get-tuple-element.181), channel_id=1, source_target_pairs={{0,112},{16,0},{32,16},{48,32},{64,48},{80,64},{96,80},{112,96},{1... | collective-permute-start | bytes 393224 | tf_op jit(solution)/shard_map/ppermute | solution.py:23
  8.8 1.0 fusion.12
  9.8 2.1 %collective-permute-done.top_ref = bf16[4,32,512]{2,1,0:T(8,128)(2,1)S(1)} collective-permute-done((bf16[4,32,512]{2,1,0:T(8,128)(2,1)S(1)}, bf16[4,32,512]{2,1,0:T(8,128)(2,1)S(1)}, u32[]{:S(2)}, u32[]{:S(2)}) %collective-permute-start) | collective-permute-done | bytes 131104 | tf_op jit(solution)/shard_map/ppermute | solution.py:23
  12.1 1.3 collective-permute-start.3
  13.5 0.6 collective-permute-start.2
  14.0 2.1 %collective-permute-done.3.right_ref = bf16[24,4,512]{2,1,0:T(4,128)(2,1)S(1)} collective-permute-done((bf16[24,4,512]{2,1,0:T(4,128)(2,1)S(1)}, bf16[24,4,512]{2,1,0:T(4,128)(2,1)S(1)}, u32[]{:S(2)}, u32[]{:S(2)}) %collective-permute-start.3) | collective-permute-done | bytes 98336 | tf_op jit(solution)/shard_map/ppermute | solution.py:23
  16.2 2.6 %collective-permute-start.4 = (bf16[1024,256]{1,0:T(8,128)(2,1)}, bf16[1024,256]{1,0:T(8,128)(2,1)}, u32[]{:S(2)}, u32[]{:S(2)}) collective-permute-start(bf16[1024,256]{1,0:T(8,128)(2,1)} %refs_8_.1), channel_id=1, source_target_pairs={{0,2},{2,0},{1,3},{3,1},{4,6},{6,4},{5,7},{7,5},{8,10},{10,8},{9,1... | collective-permute-start | bytes 1572872 | tf_op jit(solution)/shard_map/ppermute | solution.py:23
  18.8 2.8 %collective-permute-start.5 = (bf16[1024,256]{1,0:T(8,128)(2,1)}, bf16[1024,256]{1,0:T(8,128)(2,1)S(1)}, u32[]{:S(2)}, u32[]{:S(2)}) collective-permute-start(bf16[1024,256]{1,0:T(8,128)(2,1)} %refs_8_.1), channel_id=1, source_target_pairs={{0,1},{1,0},{2,3},{3,2},{4,5},{5,4},{6,7},{7,6},{8,9},{9,8},{10,11... | collective-permute-start | bytes 1572872 | tf_op jit(solution)/shard_map/ppermute | solution.py:23
  21.6 1.4 collective-permute-start.7
  23.0 1.3 collective-permute-start.8
  24.3 0.6 stack.42.place_ref.refs_0_.place
  25.0 10.2 %shard_map.145 = (bf16[128,1024]{1,0:T(8,128)(2,1)}, bf16[128,1024]{1,0:T(8,128)(2,1)}, bf16[128,2048]{1,0:T(8,128)(2,1)}, bf16[4,128,512]{2,1,0:T(8,128)(2,1)}, bf16[128,2048]{1,0:T(8,128)(2,1)}) custom-call(s32[7]{0:T(128)} %stack.42.place_ref.refs_0_.place, bf16[16,32,512]{2,1,0:T(8,128)(2,1)} %own_ref.1, bf16[4,32,512]{2,1,0:T(8,128)(2,1)} %copy-done.24, ...), custom_call_target="tpu_custom_call" | custom-call | flops 1000 | bytes 1000 | tf_op jit(solution)/shard_map/pallas_call | solution.py:168
  35.2 1.3 collective-permute-done.6.refs_5_.refs_6_
  37.5 1.2 collective-permute-start.12
  38.7 1.7 collective-permute-start.13
  40.4 0.6 collective-permute-start.10
  41.1 1.7 collective-permute-start.11
  43.1 6.4 %collective-permute-done.10.refs_2_.refs_3_ = bf16[128,1024]{1,0:T(8,128)(2,1)S(1)} collective-permute-done((bf16[128,1024]{1,0:T(8,128)(2,1)}, bf16[128,1024]{1,0:T(8,128)(2,1)S(1)}, u32[]{:S(2)}, u32[]{:S(2)}) %collective-permute-start.10) | collective-permute-done | bytes 262176 | tf_op jit(solution)/shard_map/ppermute | solution.py:23
  49.6 5.4 %collective-permute-done.11.refs_3_.refs_4_ = bf16[128,1024]{1,0:T(8,128)(2,1)S(1)} collective-permute-done((bf16[128,1024]{1,0:T(8,128)(2,1)}, bf16[128,1024]{1,0:T(8,128)(2,1)S(1)}, u32[]{:S(2)}, u32[]{:S(2)}) %collective-permute-start.11) | collective-permute-done | bytes 262176 | tf_op jit(solution)/shard_map/ppermute | solution.py:23
  54.9 1.0 collective-permute-done.9.refs_1_.refs_2_
  57.4 3.7 %all-to-all-start = ((bf16[4,128,512]{2,1,0:T(8,128)(2,1)}), bf16[4,128,512]{2,1,0:T(8,128)(2,1)S(1)}, u32[]{:S(2)}, u32[]{:S(2)}) async-start(bf16[4,128,512]{2,1,0:T(8,128)(2,1)} %get-tuple-element.121), calls=%async_computation | async-start | bytes 1048576 | tf_op jit(solution)/shard_map/all_to_all | solution.py:523
  61.1 0.8 copy-done.7
  61.9 8.6 %shard_map.146 = (bf16[128,1024]{1,0:T(8,128)(2,1)}, bf16[128,1024]{1,0:T(8,128)(2,1)}, bf16[128,1024]{1,0:T(8,128)(2,1)}, bf16[128,1024]{1,0:T(8,128)(2,1)}, bf...) custom-call(bf16[128,1024]{1,0:T(8,128)(2,1)} %get-tuple-element.103.refs_0_.refs_1_, bf16[128,1024]{1,0:T(8,128)(2,1)} %copy-done.13, ...), custom_call_target="tpu_custom_call" | custom-call | flops 1000 | bytes 1000 | tf_op jit(solution)/shard_map/pallas_call | solution.py:226
  70.5 6.1 %shard_map.147 = (bf16[16,256,256]{2,1,0:T(8,128)(2,1)}, bf16[16,256,256]{2,1,0:T(8,128)(2,1)}) custom-call(s32[7]{0:T(128)} %stack.42.place_ref.refs_0_.place, bf16[128,1024]{1,0:T(8,128)(2,1)} %get-tuple-element.103.refs_0_.refs_1_, bf16[128,1024]{1,0:T(8,128)(2,1)} %copy-done.13, bf16[128,1024]{1,0:T(8,128)(2,1)} %copy-done.11, ...), custom_call_target="tpu_custom_call" | custom-call | flops 1000 | bytes 1000 | tf_op jit(solution)/shard_map/pallas_call | solution.py:264
  76.6 0.7 collective-permute-start.16
  77.5 2.3 %collective-permute-start.17 = (bf16[128,1024]{1,0:T(8,128)(2,1)}, bf16[128,1024]{1,0:T(8,128)(2,1)S(1)}, u32[]{:S(2)}, u32[]{:S(2)}) collective-permute-start(bf16[128,1024]{1,0:T(8,128)(2,1)} %get-tuple-element.129), channel_id=1, source_target_pairs={{0,12},{4,0},{8,4},{12,8},{1,13},{5,1},{9,5},{13,9},{2,14},{6,2},{... | collective-permute-start | bytes 786440 | tf_op jit(solution)/shard_map/ppermute | solution.py:23
  79.8 0.6 collective-permute-start.18
  81.5 4.1 %shard_map.148 = bf16[16,256,256]{2,1,0:T(8,128)(2,1)} custom-call(bf16[16,256,256]{2,1,0:T(8,128)(2,1)} %get-tuple-element.124.keep, bf16[16,256,256]{2,1,0:T(8,128)(2,1)} %collective-permute-done.16.got), custom_call_target="tpu_custom_call" | custom-call | flops 1000 | bytes 1000 | tf_op jit(solution)/shard_map/pallas_call | solution.py:307
  85.5 6.9 %all-to-all-start.1 = ((bf16[16,256,256]{2,1,0:T(8,128)(2,1)}), bf16[16,256,256]{2,1,0:T(8,128)(2,1)}, u32[]{:S(2)}, u32[]{:S(2)}) async-start(bf16[16,256,256]{2,1,0:T(8,128)(2,1)} %shard_map.148), calls=%async_computation.1 | async-start | bytes 4194304 | tf_op jit(solution)/shard_map/all_to_all | solution.py:538
  92.5 3.9 %shard_map.149 = (bf16[128,1024]{1,0:T(8,128)(2,1)}, bf16[128,1024]{1,0:T(8,128)(2,1)}, bf16[128,1024]{1,0:T(8,128)(2,1)}, bf16[128,1024]{1,0:T(8,128)(2,1)}) custom-call(bf16[512,1024]{1,0:T(8,128)(2,1)} %get-tuple-element.122.refs_9_.refs_0_, bf16[256,1024]{1,0:T(8,128)(2,1)} %refs_1_.1, bf16[256,1024]{1,0:T(8,128)(2,1)} %copy-done.7, ...), custom_call_target="tpu_custom_call" | custom-call | flops 1000 | bytes 1000 | tf_op jit(solution)/shard_map/pallas_call | solution.py:337
  97.1 1.3 collective-permute-start.20
  98.3 2.2 %collective-permute-start.21 = (bf16[128,1024]{1,0:T(8,128)(2,1)S(1)}, bf16[128,1024]{1,0:T(8,128)(2,1)S(1)}, u32[]{:S(2)}, u32[]{:S(2)}) collective-permute-start(bf16[128,1024]{1,0:T(8,128)(2,1)S(1)} %fusion.8.coarse_grad.right0), channel_id=1, source_target_pairs={{0,8},{4,12},{8,0},{12,4},{1,9},{5,13},{9,1},{13,5},{2,10},{6,14},... | collective-permute-start | bytes 786440 | tf_op jit(solution)/shard_map/ppermute | solution.py:23
  100.6 1.2 collective-permute-start.22
  101.8 6.0 %shard_map.150 = (bf16[16,32,512]{2,1,0:T(8,128)(2,1)}, bf16[2,8,16,256]{3,2,1,0:T(8,128)(2,1)}, bf16[2,8,16,256]{3,2,1,0:T(8,128)(2,1)}, bf16[2,8,16,256]{3,2,1,0:T(8,128)(2,1)}, bf16[2,8,16,256]{3,2,1,0:T(8,128)(2,1)}) custom-call(s32[7]{0:T(128)} %stack.42.place_ref.refs_0_.place, bf16[128,1024]{1,0:T(8,128)(2,1)} %copy-done.3, f32[1,2048]{1,0:T(1,128)} %bitcast.31, ...), custom_call_target="tpu_custom_call" | custom-call | flops 1000 | bytes 1000 | tf_op jit(solution)/shard_map/pallas_call | solution.py:469
  108.1 0.9 collective-permute-start.25
  109.0 1.6 collective-permute-start.26
  110.5 1.4 collective-permute-done.21.right2
  112.0 0.7 copy-done.21
  112.8 3.2 %shard_map.151 = (bf16[16,16,1024]{2,1,0:T(8,128)(2,1)}, bf16[16,16,1024]{2,1,0:T(8,128)(2,1)}) custom-call(s32[7]{0:T(128)} %stack.42.place_ref.refs_0_.place, bf16[4,128,512]{2,1,0:T(8,128)(2,1)} %copy-done.5, bf16[128,1024]{1,0:T(8,128)(2,1)} %copy-done.3, bf16[128,1024]{1,0:T(8,128)(2,1)} %copy-done.20, bf16[128,1024]{1,0:T(8,128)(2,1)} %copy-done.21, ...), custom_call_target="tpu_custom_call" | custom-call | flops 1000 | bytes 1000 | tf_op jit(solution)/shard_map/pallas_call | solution.py:362
  116.0 2.6 %collective-permute-start.23 = (bf16[16,16,1024]{2,1,0:T(8,128)(2,1)}, bf16[16,16,1024]{2,1,0:T(8,128)(2,1)S(1)}, u32[]{:S(2)}, u32[]{:S(2)}) collective-permute-start(bf16[16,16,1024]{2,1,0:T(8,128)(2,1)} %get-tuple-element.147), channel_id=1, source_target_pairs={{0,1},{1,0},{2,3},{3,2},{4,5},{5,4},{6,7},{7,6},{8,9},{9,8},{10,11... | collective-permute-start | bytes 1572872 | tf_op jit(solution)/shard_map/ppermute | solution.py:23
  118.6 1.0 add_convert_fusion
  119.6 0.6 slice_bitcast_fusion
  120.7 0.9 collective-permute-done.27.proj_got
  121.6 0.6 copy-done.28
  122.4 2.2 %shard_map.152 = bf16[16,80,256]{2,1,0:T(8,128)(2,1)} custom-call(bf16[16,16,1024]{2,1,0:T(8,128)(2,1)} %get-tuple-element.146.merge_keep, bf16[16,16,1024]{2,1,0:T(8,128)(2,1)} %copy-done.17, bf16[8,16,256]{2,1,0:T(8,128)(2,1)} %get-tuple-element.184.proj_keep, bf16[8,16,256]{2,1,0:T(8,128)(2,1)} %copy-done.28), custom_call_target="tpu_custom_call" | custom-call | flops 1000 | bytes 1000 | tf_op jit(solution)/shard_map/pallas_call | solution.py:307
  124.6 19.5 %all_to_all.20.merges = bf16[16,80,256]{2,1,0:T(8,128)(2,1)} all-to-all(bf16[16,80,256]{2,1,0:T(8,128)(2,1)} %shard_map.152), channel_id=1, replica_groups=mesh['xh'=2,'z'=4,'y'=4,'xl'=2,'c'=2] {'xh','z','xl'}, dimensions={0} | all-to-all | bytes 1310720 | tf_op jit(solution)/shard_map/all_to_all | solution.py:556
  144.1 3.2 %shard_map.153 = (bf16[8,272,256]{2,1,0:T(8,128)(2,1)}, f32[16,1024]{1,0:T(8,128)}) custom-call(bf16[16,256,256]{2,1,0:T(8,128)(2,1)} %all-to-all-done.1.blocks, bf16[16,80,256]{2,1,0:T(8,128)(2,1)} %all_to_all.20.merges), custom_call_target="tpu_custom_call" | custom-call | flops 1000 | bytes 1000 | tf_op jit(solution)/shard_map/pallas_call | solution.py:307
  147.3 3.7 %all-to-all-start.3 = ((bf16[8,272,256]{2,1,0:T(8,128)(2,1)}), bf16[8,272,256]{2,1,0:T(8,128)(2,1)S(1)}, u32[]{:S(2)}, u32[]{:S(2)}) async-start(bf16[8,272,256]{2,1,0:T(8,128)(2,1)} %get-tuple-element.163), calls=%async_computation.3 | async-start | bytes 2228224 | tf_op jit(solution)/shard_map/all_to_all | solution.py:560
  151.0 1.7 collective-permute-start.28
  152.7 1.9 %collective-permute-start.29 = (bf16[128,1024]{1,0:T(8,128)(2,1)S(1)}, bf16[128,1024]{1,0:T(8,128)(2,1)S(1)}, u32[]{:S(2)}, u32[]{:S(2)}) collective-permute-start(bf16[128,1024]{1,0:T(8,128)(2,1)S(1)} %copy-done.31), channel_id=1, source_target_pairs={{0,8},{4,12},{8,0},{12,4},{1,9},{5,13},{9,1},{13,5},{2,10},{6,14},... | collective-permute-start | bytes 786440 | tf_op jit(solution)/shard_map/ppermute | solution.py:23
  154.6 3.5 %collective-permute-done.28 = bf16[128,1024]{1,0:T(8,128)(2,1)S(1)} collective-permute-done((bf16[128,1024]{1,0:T(8,128)(2,1)S(1)}, bf16[128,1024]{1,0:T(8,128)(2,1)S(1)}, u32[]{:S(2)}, u32[]{:S(2)}) %collective-permute-start.28) | collective-permute-done | bytes 262176 | tf_op jit(solution)/shard_map/ppermute | solution.py:23
  158.1 2.0 %collective-permute-done.29 = bf16[128,1024]{1,0:T(8,128)(2,1)S(1)} collective-permute-done((bf16[128,1024]{1,0:T(8,128)(2,1)S(1)}, bf16[128,1024]{1,0:T(8,128)(2,1)S(1)}, u32[]{:S(2)}, u32[]{:S(2)}) %collective-permute-start.29) | collective-permute-done | bytes 262176 | tf_op jit(solution)/shard_map/ppermute | solution.py:23
  160.1 7.6 %collective-permute-done.30 = bf16[128,1024]{1,0:T(8,128)(2,1)S(1)} collective-permute-done((bf16[128,1024]{1,0:T(8,128)(2,1)S(1)}, bf16[128,1024]{1,0:T(8,128)(2,1)S(1)}, u32[]{:S(2)}, u32[]{:S(2)}) %collective-permute-start.30) | collective-permute-done | bytes 262176 | tf_op jit(solution)/shard_map/ppermute | solution.py:23
  167.7 0.9 fusion.10
  168.7 1.4 collective-permute-start.32
  170.1 2.0 %collective-permute-start.33 = (bf16[8,16,256]{2,1,0:T(8,128)(2,1)S(1)}, bf16[8,16,256]{2,1,0:T(8,128)(2,1)S(1)}, u32[]{:S(2)}, u32[]{:S(2)}) collective-permute-start(bf16[8,16,256]{2,1,0:T(8,128)(2,1)S(1)} %get-tuple-element.178), channel_id=1, source_target_pairs={{0,12},{4,0},{8,4},{12,8},{1,13},{5,1},{9,5},{13,9},{2,14},{6,2},{... | collective-permute-start | bytes 196616 | tf_op jit(solution)/shard_map/ppermute | solution.py:23
  172.1 1.3 collective-permute-done.31
  173.4 0.8 collective-permute-done.32
  174.7 2.0 %collective-permute-start.34 = (bf16[4,8,16,256]{3,2,1,0:T(8,128)(2,1)S(1)}, bf16[4,8,16,256]{3,2,1,0:T(8,128)(2,1)S(1)}, u32[]{:S(2)}, u32[]{:S(2)}) collective-permute-start(bf16[4,8,16,256]{3,2,1,0:T(8,128)(2,1)S(1)} %pad_maximum_fusion.own), channel_id=1, source_target_pairs={{0,1},{1,0},{2,3},{3,2},{4,5},{5,4},{6,7},{7,6},{8,9},{9,8},{10,11... | collective-permute-start | bytes 786440 | tf_op jit(solution)/shard_map/ppermute | solution.py:23
  176.7 2.7 %shard_map.155 = (f32[1024,256]{1,0:T(8,128)}, f32[256,1024]{1,0:T(8,128)}) custom-call(bf16[8,272,256]{2,1,0:T(8,128)(2,1)} %copy-done.1), custom_call_target="tpu_custom_call" | custom-call | flops 1000 | bytes 1000 | tf_op jit(solution)/shard_map/pallas_call | solution.py:386
  179.5 0.7 copy-done.23
  180.2 2.1 %shard_map.154 = f32[512,512]{1,0:T(8,128)} custom-call(s32[7]{0:T(128)} %stack.42.place_ref.refs_0_.place, bf16[4,8,16,256]{3,2,1,0:T(8,128)(2,1)} %copy-done.14, bf16[4,8,16,256]{3,2,1,0:T(8,128)(2,1)} %copy-done.23), custom_call_target="tpu_custom_call" | custom-call | flops 1000 | bytes 1000 | tf_op jit(solution)/shard_map/pallas_call | solution.py:412
  (111 shorter events, 6.5 us)
Async XLA Ops:
  1.6 10.3 %collective-permute-start = (bf16[4,32,512]{2,1,0:T(8,128)(2,1)S(1)}, bf16[4,32,512]{2,1,0:T(8,128)(2,1)S(1)}, u32[]{:S(2)}, u32[]{:S(2)}) collective-permute-start(bf16[4,32,512]{2,1,0:T(8,128)(2,1)S(1)} %get-tuple-element.182), channel_id=1, source_target_pairs={{0,16},{16,32},{32,48},{48,64},{64,80},{80,96},{96,112},{112,0},{1... | collective-permute-start | bytes 393224 | tf_op jit(solution)/shard_map/ppermute | solution.py:23
  4.2 7.8 %collective-permute-start.1 = (bf16[4,32,512]{2,1,0:T(8,128)(2,1)S(1)}, bf16[4,32,512]{2,1,0:T(8,128)(2,1)S(1)}, u32[]{:S(2)}, u32[]{:S(2)}) collective-permute-start(bf16[4,32,512]{2,1,0:T(8,128)(2,1)S(1)} %get-tuple-element.181), channel_id=1, source_target_pairs={{0,112},{16,0},{32,16},{48,32},{64,48},{80,64},{96,80},{112,96},{1... | collective-permute-start | bytes 393224 | tf_op jit(solution)/shard_map/ppermute | solution.py:23
  12.0 13.0 %copy-start.24 = (bf16[4,32,512]{2,1,0:T(8,128)(2,1)}, bf16[4,32,512]{2,1,0:T(8,128)(2,1)S(1)}, u32[]{:S(2)}) copy-start(bf16[4,32,512]{2,1,0:T(8,128)(2,1)S(1)} %collective-permute-done.top_ref) | copy-start | bytes 393220
  12.0 9.6 %copy-start.25 = (bf16[4,32,512]{2,1,0:T(8,128)(2,1)}, bf16[4,32,512]{2,1,0:T(8,128)(2,1)S(1)}, u32[]{:S(2)}) copy-start(bf16[4,32,512]{2,1,0:T(8,128)(2,1)S(1)} %collective-permute-done.1.bottom_ref) | copy-start | bytes 393220
  12.1 4.1 %collective-permute-start.3 = (bf16[24,4,512]{2,1,0:T(4,128)(2,1)S(1)}, bf16[24,4,512]{2,1,0:T(4,128)(2,1)S(1)}, u32[]{:S(2)}, u32[]{:S(2)}) collective-permute-start(bf16[24,4,512]{2,1,0:T(4,128)(2,1)S(1)} %pad_maximum_fusion.2), channel_id=1, source_target_pairs={{0,15},{1,0},{2,1},{3,2},{4,3},{5,4},{6,5},{7,6},{8,7},{9,8},{10,9... | collective-permute-start | bytes 294920 | tf_op jit(solution)/shard_map/ppermute | solution.py:23
  13.5 2.8 %collective-permute-start.2 = (bf16[24,4,512]{2,1,0:T(4,128)(2,1)S(1)}, bf16[24,4,512]{2,1,0:T(4,128)(2,1)S(1)}, u32[]{:S(2)}, u32[]{:S(2)}) collective-permute-start(bf16[24,4,512]{2,1,0:T(4,128)(2,1)S(1)} %pad_maximum_fusion.1), channel_id=1, source_target_pairs={{0,1},{1,2},{2,3},{3,4},{4,5},{5,6},{6,7},{7,8},{8,9},{9,10},{10,1... | collective-permute-start | bytes 294920 | tf_op jit(solution)/shard_map/ppermute | solution.py:23
  16.2 6.8 %copy-start.26 = (bf16[24,4,512]{2,1,0:T(4,128)(2,1)}, bf16[24,4,512]{2,1,0:T(4,128)(2,1)S(1)}, u32[]{:S(2)}) copy-start(bf16[24,4,512]{2,1,0:T(4,128)(2,1)S(1)} %collective-permute-done.3.right_ref) | copy-start | bytes 294916
  16.2 8.1 %copy-start.27 = (bf16[24,4,512]{2,1,0:T(4,128)(2,1)}, bf16[24,4,512]{2,1,0:T(4,128)(2,1)S(1)}, u32[]{:S(2)}) copy-start(bf16[24,4,512]{2,1,0:T(4,128)(2,1)S(1)} %collective-permute-done.2.left_ref) | copy-start | bytes 294916
  16.2 20.6 %collective-permute-start.4 = (bf16[1024,256]{1,0:T(8,128)(2,1)}, bf16[1024,256]{1,0:T(8,128)(2,1)}, u32[]{:S(2)}, u32[]{:S(2)}) collective-permute-start(bf16[1024,256]{1,0:T(8,128)(2,1)} %refs_8_.1), channel_id=1, source_target_pairs={{0,2},{2,0},{1,3},{3,1},{4,6},{6,4},{5,7},{7,5},{8,10},{10,8},{9,1... | collective-permute-start | bytes 1572872 | tf_op jit(solution)/shard_map/ppermute | solution.py:23
  18.8 18.0 %collective-permute-start.5 = (bf16[1024,256]{1,0:T(8,128)(2,1)}, bf16[1024,256]{1,0:T(8,128)(2,1)S(1)}, u32[]{:S(2)}, u32[]{:S(2)}) collective-permute-start(bf16[1024,256]{1,0:T(8,128)(2,1)} %refs_8_.1), channel_id=1, source_target_pairs={{0,1},{1,0},{2,3},{3,2},{4,5},{5,4},{6,7},{7,6},{8,9},{9,8},{10,11... | collective-permute-start | bytes 1572872 | tf_op jit(solution)/shard_map/ppermute | solution.py:23
  21.6 14.9 %collective-permute-start.6 = (bf16[128,1024]{1,0:T(8,128)(2,1)}, bf16[128,1024]{1,0:T(8,128)(2,1)S(1)}, u32[]{:S(2)}, u32[]{:S(2)}) collective-permute-start(bf16[128,1024]{1,0:T(8,128)(2,1)} %bitcast.20), channel_id=1, source_target_pairs={{0,4},{4,8},{8,12},{12,0},{1,5},{5,9},{9,13},{13,1},{2,6},{6,10},{... | collective-permute-start | bytes 786440 | tf_op jit(solution)/shard_map/ppermute | solution.py:23
  21.6 14.9 %collective-permute-start.7 = (bf16[128,1024]{1,0:T(8,128)(2,1)}, bf16[128,1024]{1,0:T(8,128)(2,1)S(1)}, u32[]{:S(2)}, u32[]{:S(2)}) collective-permute-start(bf16[128,1024]{1,0:T(8,128)(2,1)} %bitcast.21), channel_id=1, source_target_pairs={{0,8},{4,12},{8,0},{12,4},{1,9},{5,13},{9,1},{13,5},{2,10},{6,14},... | collective-permute-start | bytes 786440 | tf_op jit(solution)/shard_map/ppermute | solution.py:23
  23.0 13.8 %collective-permute-start.8 = (bf16[128,1024]{1,0:T(8,128)(2,1)}, bf16[128,1024]{1,0:T(8,128)(2,1)S(1)}, u32[]{:S(2)}, u32[]{:S(2)}) collective-permute-start(bf16[128,1024]{1,0:T(8,128)(2,1)} %bitcast.22), channel_id=1, source_target_pairs={{0,12},{4,0},{8,4},{12,8},{1,13},{5,1},{9,5},{13,9},{2,14},{6,2},{... | collective-permute-start | bytes 786440 | tf_op jit(solution)/shard_map/ppermute | solution.py:23
  24.9 13.7 %copy-start.4 = (bf16[256,1024]{1,0:T(8,128)(2,1)S(1)}, bf16[256,1024]{1,0:T(8,128)(2,1)}, u32[]{:S(2)}) copy-start(bf16[256,1024]{1,0:T(8,128)(2,1)} %refs_1_.1) | copy-start | bytes 1572868
  36.5 25.4 %copy-start.8 = (bf16[128,1024]{1,0:T(8,128)(2,1)}, bf16[128,1024]{1,0:T(8,128)(2,1)S(1)}, u32[]{:S(2)}) copy-start(bf16[128,1024]{1,0:T(8,128)(2,1)S(1)} %collective-permute-done.6.refs_5_.refs_6_) | copy-start | bytes 786436
  36.8 1.9 %copy-start.15 = (bf16[1024,256]{1,0:T(8,128)(2,1)}, bf16[1024,256]{1,0:T(8,128)(2,1)S(1)}, u32[]{:S(2)}) copy-start(bf16[1024,256]{1,0:T(8,128)(2,1)S(1)} %collective-permute-done.5.refs_9_) | copy-start | bytes 1572868
  37.5 18.5 %collective-permute-start.12 = (bf16[1024,256]{1,0:T(8,128)(2,1)}, bf16[1024,256]{1,0:T(8,128)(2,1)S(1)}, u32[]{:S(2)}, u32[]{:S(2)}) collective-permute-start(bf16[1024,256]{1,0:T(8,128)(2,1)} %collective-permute-done.4.refs_10_), channel_id=1, source_target_pairs={{0,1},{1,0},{2,3},{3,2},{4,5},{5,4},{6,7},{7,6},{8,9},{9,8},{10,11... | collective-permute-start | bytes 1572872 | tf_op jit(solution)/shard_map/ppermute | solution.py:23
  38.7 17.3 %collective-permute-start.13 = (bf16[256,1024]{1,0:T(8,128)(2,1)S(1)}, bf16[256,1024]{1,0:T(8,128)(2,1)S(1)}, u32[]{:S(2)}, u32[]{:S(2)}) collective-permute-start(bf16[256,1024]{1,0:T(8,128)(2,1)S(1)} %copy-done.4), channel_id=1, source_target_pairs={{0,2},{2,0},{1,3},{3,1},{4,6},{6,4},{5,7},{7,5},{8,10},{10,8},{9,1... | collective-permute-start | bytes 1572872 | tf_op jit(solution)/shard_map/ppermute | solution.py:23
  40.4 9.2 %collective-permute-start.10 = (bf16[128,1024]{1,0:T(8,128)(2,1)}, bf16[128,1024]{1,0:T(8,128)(2,1)S(1)}, u32[]{:S(2)}, u32[]{:S(2)}) collective-permute-start(bf16[128,1024]{1,0:T(8,128)(2,1)} %get-tuple-element.103.refs_0_.refs_1_), channel_id=1, source_target_pairs={{0,8},{4,12},{8,0},{12,4},{1,9},{5,13},{9,1},{13,5},{2,10},{6,14},... | collective-permute-start | bytes 786440 | tf_op jit(solution)/shard_map/ppermute | solution.py:23
  41.1 13.9 %collective-permute-start.11 = (bf16[128,1024]{1,0:T(8,128)(2,1)}, bf16[128,1024]{1,0:T(8,128)(2,1)S(1)}, u32[]{:S(2)}, u32[]{:S(2)}) collective-permute-start(bf16[128,1024]{1,0:T(8,128)(2,1)} %get-tuple-element.103.refs_0_.refs_1_), channel_id=1, source_target_pairs={{0,12},{4,0},{8,4},{12,8},{1,13},{5,1},{9,5},{13,9},{2,14},{6,2},{... | collective-permute-start | bytes 786440 | tf_op jit(solution)/shard_map/ppermute | solution.py:23
  42.8 13.2 %collective-permute-start.9 = (bf16[128,1024]{1,0:T(8,128)(2,1)}, bf16[128,1024]{1,0:T(8,128)(2,1)S(1)}, u32[]{:S(2)}, u32[]{:S(2)}) collective-permute-start(bf16[128,1024]{1,0:T(8,128)(2,1)} %get-tuple-element.103.refs_0_.refs_1_), channel_id=1, source_target_pairs={{0,4},{4,8},{8,12},{12,0},{1,5},{5,9},{9,13},{13,1},{2,6},{6,10},{... | collective-permute-start | bytes 786440 | tf_op jit(solution)/shard_map/ppermute | solution.py:23
  49.6 7.8 %copy-start.11 = (bf16[128,1024]{1,0:T(8,128)(2,1)}, bf16[128,1024]{1,0:T(8,128)(2,1)S(1)}, u32[]{:S(2)}) copy-start(bf16[128,1024]{1,0:T(8,128)(2,1)S(1)} %collective-permute-done.10.refs_2_.refs_3_) | copy-start | bytes 786436
  54.9 2.4 %copy-start.12 = (bf16[128,1024]{1,0:T(8,128)(2,1)}, bf16[128,1024]{1,0:T(8,128)(2,1)S(1)}, u32[]{:S(2)}) copy-start(bf16[128,1024]{1,0:T(8,128)(2,1)S(1)} %collective-permute-done.11.refs_3_.refs_4_) | copy-start | bytes 786436
  56.0 0.9 copy-start.16
  56.0 5.9 %copy-start.6 = (bf16[256,1024]{1,0:T(8,128)(2,1)}, bf16[256,1024]{1,0:T(8,128)(2,1)S(1)}, u32[]{:S(2)}) copy-start(bf16[256,1024]{1,0:T(8,128)(2,1)S(1)} %collective-permute-done.13.refs_14_.refs_3_) | copy-start | bytes 1572868
  56.0 5.0 %collective-permute-start.14 = (bf16[256,1024]{1,0:T(8,128)(2,1)S(1)}, bf16[256,1024]{1,0:T(8,128)(2,1)S(1)}, u32[]{:S(2)}, u32[]{:S(2)}) collective-permute-start(bf16[256,1024]{1,0:T(8,128)(2,1)S(1)} %copy-done.4), channel_id=1, source_target_pairs={{0,1},{1,0},{2,3},{3,2},{4,5},{5,4},{6,7},{7,6},{8,9},{9,8},{10,11... | collective-permute-start | bytes 1572872 | tf_op jit(solution)/shard_map/ppermute | solution.py:23
  56.9 5.0 %collective-permute-start.15 = (bf16[256,1024]{1,0:T(8,128)(2,1)S(1)}, bf16[256,1024]{1,0:T(8,128)(2,1)}, u32[]{:S(2)}, u32[]{:S(2)}) collective-permute-start(bf16[256,1024]{1,0:T(8,128)(2,1)S(1)} %collective-permute-done.13.refs_14_.refs_3_), channel_id=1, source_target_pairs={{0,1},{1,0},{2,3},{3,2},{4,5},{5,4},{6,7},{7,6},{8,9},{9,8},{10,11... | collective-permute-start | bytes 1572872 | tf_op jit(solution)/shard_map/ppermute | solution.py:23
  57.4 13.1 %all-to-all-start = ((bf16[4,128,512]{2,1,0:T(8,128)(2,1)}), bf16[4,128,512]{2,1,0:T(8,128)(2,1)S(1)}, u32[]{:S(2)}, u32[]{:S(2)}) async-start(bf16[4,128,512]{2,1,0:T(8,128)(2,1)} %get-tuple-element.121), calls=%async_computation | async-start | bytes 1048576 | tf_op jit(solution)/shard_map/all_to_all | solution.py:523
  61.0 0.8 copy-start.7
  70.5 6.1 %copy-start.5 = (bf16[4,128,512]{2,1,0:T(8,128)(2,1)}, bf16[4,128,512]{2,1,0:T(8,128)(2,1)S(1)}, u32[]{:S(2)}) copy-start(bf16[4,128,512]{2,1,0:T(8,128)(2,1)S(1)} %all-to-all-done.left) | copy-start | bytes 1572868
  70.5 6.9 %copy-start = (bf16[128,1024]{1,0:T(8,128)(2,1)S(1)}, bf16[128,1024]{1,0:T(8,128)(2,1)}, u32[]{:S(2)}) copy-start(bf16[128,1024]{1,0:T(8,128)(2,1)} %get-tuple-element.127) | copy-start | bytes 786436
  70.5 9.9 %copy-start.33 = (bf16[128,1024]{1,0:T(8,128)(2,1)S(1)}, bf16[128,1024]{1,0:T(8,128)(2,1)}, u32[]{:S(2)}) copy-start(bf16[128,1024]{1,0:T(8,128)(2,1)} %get-tuple-element.131) | copy-start | bytes 786436
  76.6 4.9 %collective-permute-start.16 = (bf16[16,256,256]{2,1,0:T(8,128)(2,1)}, bf16[16,256,256]{2,1,0:T(8,128)(2,1)}, u32[]{:S(2)}, u32[]{:S(2)}) collective-permute-start(bf16[16,256,256]{2,1,0:T(8,128)(2,1)} %get-tuple-element.125), channel_id=1, source_target_pairs={{0,1},{1,0},{2,3},{3,2},{4,5},{5,4},{6,7},{7,6},{8,9},{9,8},{10,11... | collective-permute-start | bytes 6291464 | tf_op jit(solution)/shard_map/ppermute | solution.py:23
  77.5 18.9 %collective-permute-start.17 = (bf16[128,1024]{1,0:T(8,128)(2,1)}, bf16[128,1024]{1,0:T(8,128)(2,1)S(1)}, u32[]{:S(2)}, u32[]{:S(2)}) collective-permute-start(bf16[128,1024]{1,0:T(8,128)(2,1)} %get-tuple-element.129), channel_id=1, source_target_pairs={{0,12},{4,0},{8,4},{12,8},{1,13},{5,1},{9,5},{13,9},{2,14},{6,2},{... | collective-permute-start | bytes 786440 | tf_op jit(solution)/shard_map/ppermute | solution.py:23
  79.8 16.6 %collective-permute-start.18 = (bf16[128,1024]{1,0:T(8,128)(2,1)}, bf16[128,1024]{1,0:T(8,128)(2,1)S(1)}, u32[]{:S(2)}, u32[]{:S(2)}) collective-permute-start(bf16[128,1024]{1,0:T(8,128)(2,1)} %get-tuple-element.130), channel_id=1, source_target_pairs={{0,8},{4,12},{8,0},{12,4},{1,9},{5,13},{9,1},{13,5},{2,10},{6,14},... | collective-permute-start | bytes 786440 | tf_op jit(solution)/shard_map/ppermute | solution.py:23
  80.4 16.0 %collective-permute-start.19 = (bf16[128,1024]{1,0:T(8,128)(2,1)S(1)}, bf16[128,1024]{1,0:T(8,128)(2,1)S(1)}, u32[]{:S(2)}, u32[]{:S(2)}) collective-permute-start(bf16[128,1024]{1,0:T(8,128)(2,1)S(1)} %copy-done.33), channel_id=1, source_target_pairs={{0,4},{4,8},{8,12},{12,0},{1,5},{5,9},{9,13},{13,1},{2,6},{6,10},{... | collective-permute-start | bytes 786440 | tf_op jit(solution)/shard_map/ppermute | solution.py:23
  85.5 39.1 %all-to-all-start.1 = ((bf16[16,256,256]{2,1,0:T(8,128)(2,1)}), bf16[16,256,256]{2,1,0:T(8,128)(2,1)}, u32[]{:S(2)}, u32[]{:S(2)}) async-start(bf16[16,256,256]{2,1,0:T(8,128)(2,1)} %shard_map.148), calls=%async_computation.1 | async-start | bytes 4194304 | tf_op jit(solution)/shard_map/all_to_all | solution.py:538
  92.5 3.9 %copy-start.19 = (bf16[128,1024]{1,0:T(8,128)(2,1)S(1)}, bf16[128,1024]{1,0:T(8,128)(2,1)}, u32[]{:S(2)}) copy-start(bf16[128,1024]{1,0:T(8,128)(2,1)} %get-tuple-element.128) | copy-start | bytes 786436
  92.5 3.9 %copy-start.29 = (f32[1024]{0:T(1024)S(1)}, f32[1024]{0:T(1024)}, u32[]{:S(2)}) copy-start(f32[1024]{0:T(1024)} %param.16) | copy-start | bytes 12292
  92.5 4.3 %copy-start.2 = (bf16[8,16,1024]{2,1,0:T(8,128)(2,1)S(1)}, bf16[8,16,1024]{2,1,0:T(8,128)(2,1)}, u32[]{:S(2)}) copy-start(bf16[8,16,1024]{2,1,0:T(8,128)(2,1)} %param.19) | copy-start | bytes 786436
  97.1 4.7 %copy-start.3 = (bf16[128,1024]{1,0:T(8,128)(2,1)}, bf16[128,1024]{1,0:T(8,128)(2,1)S(1)}, u32[]{:S(2)}) copy-start(bf16[128,1024]{1,0:T(8,128)(2,1)S(1)} %fusion.8.coarse_grad.right0) | copy-start | bytes 786436
  97.1 11.9 %collective-permute-start.20 = (bf16[128,1024]{1,0:T(8,128)(2,1)S(1)}, bf16[128,1024]{1,0:T(8,128)(2,1)S(1)}, u32[]{:S(2)}, u32[]{:S(2)}) collective-permute-start(bf16[128,1024]{1,0:T(8,128)(2,1)S(1)} %fusion.8.coarse_grad.right0), channel_id=1, source_target_pairs={{0,4},{4,8},{8,12},{12,0},{1,5},{5,9},{9,13},{13,1},{2,6},{6,10},{... | collective-permute-start | bytes 786440 | tf_op jit(solution)/shard_map/ppermute | solution.py:23
  98.3 13.7 %collective-permute-start.21 = (bf16[128,1024]{1,0:T(8,128)(2,1)S(1)}, bf16[128,1024]{1,0:T(8,128)(2,1)S(1)}, u32[]{:S(2)}, u32[]{:S(2)}) collective-permute-start(bf16[128,1024]{1,0:T(8,128)(2,1)S(1)} %fusion.8.coarse_grad.right0), channel_id=1, source_target_pairs={{0,8},{4,12},{8,0},{12,4},{1,9},{5,13},{9,1},{13,5},{2,10},{6,14},... | collective-permute-start | bytes 786440 | tf_op jit(solution)/shard_map/ppermute | solution.py:23
  100.6 11.4 %collective-permute-start.22 = (bf16[128,1024]{1,0:T(8,128)(2,1)S(1)}, bf16[128,1024]{1,0:T(8,128)(2,1)S(1)}, u32[]{:S(2)}, u32[]{:S(2)}) collective-permute-start(bf16[128,1024]{1,0:T(8,128)(2,1)S(1)} %fusion.8.coarse_grad.right0), channel_id=1, source_target_pairs={{0,12},{4,0},{8,4},{12,8},{1,13},{5,1},{9,5},{13,9},{2,14},{6,2},{... | collective-permute-start | bytes 786440 | tf_op jit(solution)/shard_map/ppermute | solution.py:23
  107.8 10.8 %collective-permute-start.24 = (bf16[2,8,16,256]{3,2,1,0:T(8,128)(2,1)}, bf16[2,8,16,256]{3,2,1,0:T(8,128)(2,1)S(1)}, u32[]{:S(2)}, u32[]{:S(2)}) collective-permute-start(bf16[2,8,16,256]{3,2,1,0:T(8,128)(2,1)} %get-tuple-element.149), channel_id=1, source_target_pairs={{0,4},{4,8},{8,12},{12,0},{1,5},{5,9},{9,13},{13,1},{2,6},{6,10},{... | collective-permute-start | bytes 393224 | tf_op jit(solution)/shard_map/ppermute | solution.py:23
  108.1 10.5 %collective-permute-start.25 = (bf16[2,8,16,256]{3,2,1,0:T(8,128)(2,1)}, bf16[2,8,16,256]{3,2,1,0:T(8,128)(2,1)S(1)}, u32[]{:S(2)}, u32[]{:S(2)}) collective-permute-start(bf16[2,8,16,256]{3,2,1,0:T(8,128)(2,1)} %get-tuple-element.150), channel_id=1, source_target_pairs={{0,8},{4,12},{8,0},{12,4},{1,9},{5,13},{9,1},{13,5},{2,10},{6,14},... | collective-permute-start | bytes 393224 | tf_op jit(solution)/shard_map/ppermute | solution.py:23
  109.0 3.0 %copy-start.20 = (bf16[128,1024]{1,0:T(8,128)(2,1)}, bf16[128,1024]{1,0:T(8,128)(2,1)S(1)}, u32[]{:S(2)}) copy-start(bf16[128,1024]{1,0:T(8,128)(2,1)S(1)} %collective-permute-done.20.right1) | copy-start | bytes 786436
  109.0 9.6 %collective-permute-start.26 = (bf16[2,8,16,256]{3,2,1,0:T(8,128)(2,1)}, bf16[2,8,16,256]{3,2,1,0:T(8,128)(2,1)S(1)}, u32[]{:S(2)}, u32[]{:S(2)}) collective-permute-start(bf16[2,8,16,256]{3,2,1,0:T(8,128)(2,1)} %get-tuple-element.151), channel_id=1, source_target_pairs={{0,12},{4,0},{8,4},{12,8},{1,13},{5,1},{9,5},{13,9},{2,14},{6,2},{... | collective-permute-start | bytes 393224 | tf_op jit(solution)/shard_map/ppermute | solution.py:23
  116.0 5.6 %collective-permute-start.23 = (bf16[16,16,1024]{2,1,0:T(8,128)(2,1)}, bf16[16,16,1024]{2,1,0:T(8,128)(2,1)S(1)}, u32[]{:S(2)}, u32[]{:S(2)}) collective-permute-start(bf16[16,16,1024]{2,1,0:T(8,128)(2,1)} %get-tuple-element.147), channel_id=1, source_target_pairs={{0,1},{1,0},{2,3},{3,2},{4,5},{5,4},{6,7},{7,6},{8,9},{9,8},{10,11... | collective-permute-start | bytes 1572872 | tf_op jit(solution)/shard_map/ppermute | solution.py:23
  120.2 1.4 collective-permute-start.27
  144.1 10.5 %copy-start.30 = (bf16[128,1024]{1,0:T(8,128)(2,1)S(1)}, bf16[128,1024]{1,0:T(8,128)(2,1)}, u32[]{:S(2)}) copy-start(bf16[128,1024]{1,0:T(8,128)(2,1)} %get-tuple-element.167) | copy-start | bytes 786436
  144.1 23.6 %copy-start.18 = (bf16[128,1024]{1,0:T(8,128)(2,1)S(1)}, bf16[128,1024]{1,0:T(8,128)(2,1)}, u32[]{:S(2)}) copy-start(bf16[128,1024]{1,0:T(8,128)(2,1)} %get-tuple-element.164) | copy-start | bytes 786436
  147.3 3.7 %copy-start.32 = (bf16[128,1024]{1,0:T(8,128)(2,1)S(1)}, bf16[128,1024]{1,0:T(8,128)(2,1)}, u32[]{:S(2)}) copy-start(bf16[128,1024]{1,0:T(8,128)(2,1)} %get-tuple-element.165) | copy-start | bytes 786436
  147.3 5.4 %copy-start.31 = (bf16[128,1024]{1,0:T(8,128)(2,1)S(1)}, bf16[128,1024]{1,0:T(8,128)(2,1)}, u32[]{:S(2)}) copy-start(bf16[128,1024]{1,0:T(8,128)(2,1)} %get-tuple-element.166) | copy-start | bytes 786436
  147.3 21.4 %all-to-all-start.3 = ((bf16[8,272,256]{2,1,0:T(8,128)(2,1)}), bf16[8,272,256]{2,1,0:T(8,128)(2,1)S(1)}, u32[]{:S(2)}, u32[]{:S(2)}) async-start(bf16[8,272,256]{2,1,0:T(8,128)(2,1)} %get-tuple-element.163), calls=%async_computation.3 | async-start | bytes 2228224 | tf_op jit(solution)/shard_map/all_to_all | solution.py:560
  151.0 7.1 %collective-permute-start.28 = (bf16[128,1024]{1,0:T(8,128)(2,1)S(1)}, bf16[128,1024]{1,0:T(8,128)(2,1)S(1)}, u32[]{:S(2)}, u32[]{:S(2)}) collective-permute-start(bf16[128,1024]{1,0:T(8,128)(2,1)S(1)} %copy-done.32), channel_id=1, source_target_pairs={{0,12},{4,0},{8,4},{12,8},{1,13},{5,1},{9,5},{13,9},{2,14},{6,2},{... | collective-permute-start | bytes 786440 | tf_op jit(solution)/shard_map/ppermute | solution.py:23
  152.7 7.4 %collective-permute-start.29 = (bf16[128,1024]{1,0:T(8,128)(2,1)S(1)}, bf16[128,1024]{1,0:T(8,128)(2,1)S(1)}, u32[]{:S(2)}, u32[]{:S(2)}) collective-permute-start(bf16[128,1024]{1,0:T(8,128)(2,1)S(1)} %copy-done.31), channel_id=1, source_target_pairs={{0,8},{4,12},{8,0},{12,4},{1,9},{5,13},{9,1},{13,5},{2,10},{6,14},... | collective-permute-start | bytes 786440 | tf_op jit(solution)/shard_map/ppermute | solution.py:23
  154.6 13.1 %collective-permute-start.30 = (bf16[128,1024]{1,0:T(8,128)(2,1)S(1)}, bf16[128,1024]{1,0:T(8,128)(2,1)S(1)}, u32[]{:S(2)}, u32[]{:S(2)}) collective-permute-start(bf16[128,1024]{1,0:T(8,128)(2,1)S(1)} %copy-done.30), channel_id=1, source_target_pairs={{0,4},{4,8},{8,12},{12,0},{1,5},{5,9},{9,13},{13,1},{2,6},{6,10},{... | collective-permute-start | bytes 786440 | tf_op jit(solution)/shard_map/ppermute | solution.py:23
  168.6 8.1 %copy-start.1 = (bf16[8,272,256]{2,1,0:T(8,128)(2,1)}, bf16[8,272,256]{2,1,0:T(8,128)(2,1)S(1)}, u32[]{:S(2)}) copy-start(bf16[8,272,256]{2,1,0:T(8,128)(2,1)S(1)} %all-to-all-done.3.blocks) | copy-start | bytes 3342340
  168.7 4.7 %collective-permute-start.31 = (bf16[8,16,256]{2,1,0:T(8,128)(2,1)S(1)}, bf16[8,16,256]{2,1,0:T(8,128)(2,1)S(1)}, u32[]{:S(2)}, u32[]{:S(2)}) collective-permute-start(bf16[8,16,256]{2,1,0:T(8,128)(2,1)S(1)} %get-tuple-element.178), channel_id=1, source_target_pairs={{0,4},{4,8},{8,12},{12,0},{1,5},{5,9},{9,13},{13,1},{2,6},{6,10},{... | collective-permute-start | bytes 196616 | tf_op jit(solution)/shard_map/ppermute | solution.py:23
  168.7 5.5 %collective-permute-start.32 = (bf16[8,16,256]{2,1,0:T(8,128)(2,1)S(1)}, bf16[8,16,256]{2,1,0:T(8,128)(2,1)S(1)}, u32[]{:S(2)}, u32[]{:S(2)}) collective-permute-start(bf16[8,16,256]{2,1,0:T(8,128)(2,1)S(1)} %get-tuple-element.178), channel_id=1, source_target_pairs={{0,8},{4,12},{8,0},{12,4},{1,9},{5,13},{9,1},{13,5},{2,10},{6,14},... | collective-permute-start | bytes 196616 | tf_op jit(solution)/shard_map/ppermute | solution.py:23
  170.1 4.5 %collective-permute-start.33 = (bf16[8,16,256]{2,1,0:T(8,128)(2,1)S(1)}, bf16[8,16,256]{2,1,0:T(8,128)(2,1)S(1)}, u32[]{:S(2)}, u32[]{:S(2)}) collective-permute-start(bf16[8,16,256]{2,1,0:T(8,128)(2,1)S(1)} %get-tuple-element.178), channel_id=1, source_target_pairs={{0,12},{4,0},{8,4},{12,8},{1,13},{5,1},{9,5},{13,9},{2,14},{6,2},{... | collective-permute-start | bytes 196616 | tf_op jit(solution)/shard_map/ppermute | solution.py:23
  174.7 4.8 %copy-start.14 = (bf16[4,8,16,256]{3,2,1,0:T(8,128)(2,1)}, bf16[4,8,16,256]{3,2,1,0:T(8,128)(2,1)S(1)}, u32[]{:S(2)}) copy-start(bf16[4,8,16,256]{3,2,1,0:T(8,128)(2,1)S(1)} %pad_maximum_fusion.own) | copy-start | bytes 786436
  174.7 4.8 %collective-permute-start.34 = (bf16[4,8,16,256]{3,2,1,0:T(8,128)(2,1)S(1)}, bf16[4,8,16,256]{3,2,1,0:T(8,128)(2,1)S(1)}, u32[]{:S(2)}, u32[]{:S(2)}) collective-permute-start(bf16[4,8,16,256]{3,2,1,0:T(8,128)(2,1)S(1)} %pad_maximum_fusion.own), channel_id=1, source_target_pairs={{0,1},{1,0},{2,3},{3,2},{4,5},{5,4},{6,7},{7,6},{8,9},{9,8},{10,11... | collective-permute-start | bytes 786440 | tf_op jit(solution)/shard_map/ppermute | solution.py:23
  (8 other events, 5.8 us)
where the time goes:
time: 183 us; the launch traced here: 182 us
  starting transfers between devices  62 us (34%)
  Pallas kernels  52.2 us (29%)
  waiting for transfers between devices  37 us (20%)
  blocking collectives  19.5 us (11%)
  local copies, waits for them, and re-layouts  7.53 us (4%)
  other arithmetic  3.03 us (2%)
    ppermute x35, starting transfers between devices, rotate(): lax.ppermute(value, axis, [(i, (i + shift) % size) for i in range(size)])  47.8 us
    ppermute x35, waiting for transfers between devices, rotate(): lax.ppermute(value, axis, [(i, (i + shift) % size) for i in range(size)])  37 us
    all_to_all x1, blocking collectives, per_device(): merges = lax.all_to_all(merges, LAT + ('xl',), 0, 0)  19.5 us
    pallas_call x1, Pallas kernels, attend(): pl.pallas_call(attend_kernel, out_shape=shapes, in_specs=[SMEM] + [VMEM]...  10.2 us
    pallas_call x3, Pallas kernels, sums(): pl.pallas_call(kernel, out_shape=[jax.ShapeDtypeStruct(shape, F32 if shap...  9.4 us
    pallas_call x1, Pallas kernels, hidden_units(): pl.pallas_call(hidden_kernel, out_shape=out, in_specs=[VMEM] * 16, out_sp...  8.59 us
    all_to_all x1, starting transfers between devices, per_device(): blocks = lax.all_to_all(blocks, LAT + ('xl',), 0, 0)  6.91 us
    pallas_call x1, Pallas kernels, weight_grads(): pl.pallas_call(weight_grad_kernel, out_shape=[jax.ShapeDtypeStruct((16, 2...  6.1 us
  transfers between devices with their start and end apart: 38, of which 16 were waited for; matrix products, arithmetic and copies ran while one was open for 3% of the time, Pallas kernels for 22%

commit v1 on v0

--- a/solution.py
+++ b/solution.py
@@ -564,6 +564,7 @@
 
     proj = jnp.stack(gather_rel(blocks[:, 256:], "y"))
     grad_up, grad_down = place_blocks(blocks)
+    proj, grad_up = together(proj, grad_up)
     grad_proj = place_proj(place, proj, rotate(proj, "c", 1))
 
     level_two = level_two.reshape(tile_rows // 2, tile_cols // 2, width)

time: 183 us -> 181 us (0.989)
  transfers between devices with their start and end apart: 38 -> 38, of which waited for: 16 -> 14; matrix products, arithmetic and copies ran while one was open for 3% -> 3% of each run, Pallas kernels for 22% -> 23%
where the time goes in v1:
time: 181 us
  starting transfers between devices  61.9 us (34%)
  Pallas kernels  52.2 us (29%)
  waiting for transfers between devices  35.7 us (20%)
  blocking collectives  19.5 us (11%)
  local copies, waits for them, and re-layouts  7.51 us (4%)
  other arithmetic  3.03 us (2%)
    ppermute x35, starting transfers between devices, rotate(): lax.ppermute(value, axis, [(i, (i + shift) % size) for i in range(size)])  47.6 us
    ppermute x35, waiting for transfers between devices, rotate(): lax.ppermute(value, axis, [(i, (i + shift) % size) for i in range(size)])  35.7 us
    all_to_all x1, blocking collectives, per_device(): merges = lax.all_to_all(merges, LAT + ('xl',), 0, 0)  19.5 us
    pallas_call x1, Pallas kernels, attend(): pl.pallas_call(attend_kernel, out_shape=shapes, in_specs=[SMEM] + [VMEM]...  10.2 us
    pallas_call x3, Pallas kernels, sums(): pl.pallas_call(kernel, out_shape=[jax.ShapeDtypeStruct(shape, F32 if shap...  9.4 us
    pallas_call x1, Pallas kernels, hidden_units(): pl.pallas_call(hidden_kernel, out_shape=out, in_specs=[VMEM] * 16, out_sp...  8.59 us
    all_to_all x1, starting transfers between devices, per_device(): blocks = lax.all_to_all(blocks, LAT + ('xl',), 0, 0)  6.91 us
    pallas_call x1, Pallas kernels, weight_grads(): pl.pallas_call(weight_grad_kernel, out_shape=[jax.ShapeDtypeStruct((16, 2...  6.1 us
  transfers between devices with their start and end apart: 38, of which 14 were waited for; matrix products, arithmetic and copies ran while one was open for 3% of the time, Pallas kernels for 23%

profile of v1, /device:TPU:1, one launch (start us, length us, event | category | flops | bytes accessed | tf_op | source)
XLA Modules:
  0.0 180.8 jit_solution(18020291861367127131)
XLA Ops:
  0.6 1.0 fusion.13
  1.6 2.5 %collective-permute-start = (bf16[4,32,512]{2,1,0:T(8,128)(2,1)S(1)}, bf16[4,32,512]{2,1,0:T(8,128)(2,1)S(1)}, u32[]{:S(2)}, u32[]{:S(2)}) collective-permute-start(bf16[4,32,512]{2,1,0:T(8,128)(2,1)S(1)} %get-tuple-element.186), channel_id=1, source_target_pairs={{0,16},{16,32},{32,48},{48,64},{64,80},{80,96},{96,112},{112,0},{1... | collective-permute-start | bytes 393224 | tf_op jit(solution)/shard_map/ppermute | solution.py:23
  4.2 4.7 %collective-permute-start.1 = (bf16[4,32,512]{2,1,0:T(8,128)(2,1)S(1)}, bf16[4,32,512]{2,1,0:T(8,128)(2,1)S(1)}, u32[]{:S(2)}, u32[]{:S(2)}) collective-permute-start(bf16[4,32,512]{2,1,0:T(8,128)(2,1)S(1)} %get-tuple-element.185), channel_id=1, source_target_pairs={{0,112},{16,0},{32,16},{48,32},{64,48},{80,64},{96,80},{112,96},{1... | collective-permute-start | bytes 393224 | tf_op jit(solution)/shard_map/ppermute | solution.py:23
  8.8 1.0 fusion.12
  9.8 2.1 %collective-permute-done.top_ref = bf16[4,32,512]{2,1,0:T(8,128)(2,1)S(1)} collective-permute-done((bf16[4,32,512]{2,1,0:T(8,128)(2,1)S(1)}, bf16[4,32,512]{2,1,0:T(8,128)(2,1)S(1)}, u32[]{:S(2)}, u32[]{:S(2)}) %collective-permute-start) | collective-permute-done | bytes 131104 | tf_op jit(solution)/shard_map/ppermute | solution.py:23
  12.1 1.3 collective-permute-start.3
  13.5 0.6 collective-permute-start.2
  14.0 2.1 %collective-permute-done.3.right_ref = bf16[24,4,512]{2,1,0:T(4,128)(2,1)S(1)} collective-permute-done((bf16[24,4,512]{2,1,0:T(4,128)(2,1)S(1)}, bf16[24,4,512]{2,1,0:T(4,128)(2,1)S(1)}, u32[]{:S(2)}, u32[]{:S(2)}) %collective-permute-start.3) | collective-permute-done | bytes 98336 | tf_op jit(solution)/shard_map/ppermute | solution.py:23
  16.2 2.6 %collective-permute-start.4 = (bf16[1024,256]{1,0:T(8,128)(2,1)}, bf16[1024,256]{1,0:T(8,128)(2,1)}, u32[]{:S(2)}, u32[]{:S(2)}) collective-permute-start(bf16[1024,256]{1,0:T(8,128)(2,1)} %refs_8_.1), channel_id=1, source_target_pairs={{0,2},{2,0},{1,3},{3,1},{4,6},{6,4},{5,7},{7,5},{8,10},{10,8},{9,1... | collective-permute-start | bytes 1572872 | tf_op jit(solution)/shard_map/ppermute | solution.py:23
  18.8 2.8 %collective-permute-start.5 = (bf16[1024,256]{1,0:T(8,128)(2,1)}, bf16[1024,256]{1,0:T(8,128)(2,1)S(1)}, u32[]{:S(2)}, u32[]{:S(2)}) collective-permute-start(bf16[1024,256]{1,0:T(8,128)(2,1)} %refs_8_.1), channel_id=1, source_target_pairs={{0,1},{1,0},{2,3},{3,2},{4,5},{5,4},{6,7},{7,6},{8,9},{9,8},{10,11... | collective-permute-start | bytes 1572872 | tf_op jit(solution)/shard_map/ppermute | solution.py:23
  21.6 1.4 collective-permute-start.7
  23.0 1.3 collective-permute-start.8
  24.3 0.6 stack.42.place_ref.refs_0_.place
  25.0 10.2 %shard_map.145 = (bf16[128,1024]{1,0:T(8,128)(2,1)}, bf16[128,1024]{1,0:T(8,128)(2,1)}, bf16[128,2048]{1,0:T(8,128)(2,1)}, bf16[4,128,512]{2,1,0:T(8,128)(2,1)}, bf16[128,2048]{1,0:T(8,128)(2,1)}) custom-call(s32[7]{0:T(128)} %stack.42.place_ref.refs_0_.place, bf16[16,32,512]{2,1,0:T(8,128)(2,1)} %own_ref.1, bf16[4,32,512]{2,1,0:T(8,128)(2,1)} %copy-done.24, ...), custom_call_target="tpu_custom_call" | custom-call | flops 1000 | bytes 1000 | tf_op jit(solution)/shard_map/pallas_call | solution.py:168
  35.2 1.3 collective-permute-done.6.refs_5_.refs_6_
  37.5 1.2 collective-permute-start.12
  38.7 1.7 collective-permute-start.13
  40.4 0.6 collective-permute-start.10
  41.1 1.7 collective-permute-start.11
  43.1 6.4 %collective-permute-done.10.refs_2_.refs_3_ = bf16[128,1024]{1,0:T(8,128)(2,1)S(1)} collective-permute-done((bf16[128,1024]{1,0:T(8,128)(2,1)}, bf16[128,1024]{1,0:T(8,128)(2,1)S(1)}, u32[]{:S(2)}, u32[]{:S(2)}) %collective-permute-start.10) | collective-permute-done | bytes 262176 | tf_op jit(solution)/shard_map/ppermute | solution.py:23
  49.6 5.4 %collective-permute-done.11.refs_3_.refs_4_ = bf16[128,1024]{1,0:T(8,128)(2,1)S(1)} collective-permute-done((bf16[128,1024]{1,0:T(8,128)(2,1)}, bf16[128,1024]{1,0:T(8,128)(2,1)S(1)}, u32[]{:S(2)}, u32[]{:S(2)}) %collective-permute-start.11) | collective-permute-done | bytes 262176 | tf_op jit(solution)/shard_map/ppermute | solution.py:23
  54.9 1.0 collective-permute-done.9.refs_1_.refs_2_
  56.0 0.6 collective-permute-start.14
  57.4 3.7 %all-to-all-start = ((bf16[4,128,512]{2,1,0:T(8,128)(2,1)}), bf16[4,128,512]{2,1,0:T(8,128)(2,1)S(1)}, u32[]{:S(2)}, u32[]{:S(2)}) async-start(bf16[4,128,512]{2,1,0:T(8,128)(2,1)} %get-tuple-element.123), calls=%async_computation | async-start | bytes 1048576 | tf_op jit(solution)/shard_map/all_to_all | solution.py:523
  61.1 0.8 copy-done.7
  61.9 8.6 %shard_map.146 = (bf16[128,1024]{1,0:T(8,128)(2,1)}, bf16[128,1024]{1,0:T(8,128)(2,1)}, bf16[128,1024]{1,0:T(8,128)(2,1)}, bf16[128,1024]{1,0:T(8,128)(2,1)}, bf...) custom-call(bf16[128,1024]{1,0:T(8,128)(2,1)} %get-tuple-element.105.refs_0_.refs_1_, bf16[128,1024]{1,0:T(8,128)(2,1)} %copy-done.13, ...), custom_call_target="tpu_custom_call" | custom-call | flops 1000 | bytes 1000 | tf_op jit(solution)/shard_map/pallas_call | solution.py:226
  70.5 6.1 %shard_map.147 = (bf16[16,256,256]{2,1,0:T(8,128)(2,1)}, bf16[16,256,256]{2,1,0:T(8,128)(2,1)}) custom-call(s32[7]{0:T(128)} %stack.42.place_ref.refs_0_.place, bf16[128,1024]{1,0:T(8,128)(2,1)} %get-tuple-element.105.refs_0_.refs_1_, bf16[128,1024]{1,0:T(8,128)(2,1)} %copy-done.13, bf16[128,1024]{1,0:T(8,128)(2,1)} %copy-done.11, ...), custom_call_target="tpu_custom_call" | custom-call | flops 1000 | bytes 1000 | tf_op jit(solution)/shard_map/pallas_call | solution.py:264
  76.6 0.7 collective-permute-start.16
  77.5 2.3 %collective-permute-start.17 = (bf16[128,1024]{1,0:T(8,128)(2,1)}, bf16[128,1024]{1,0:T(8,128)(2,1)S(1)}, u32[]{:S(2)}, u32[]{:S(2)}) collective-permute-start(bf16[128,1024]{1,0:T(8,128)(2,1)} %get-tuple-element.131), channel_id=1, source_target_pairs={{0,12},{4,0},{8,4},{12,8},{1,13},{5,1},{9,5},{13,9},{2,14},{6,2},{... | collective-permute-start | bytes 786440 | tf_op jit(solution)/shard_map/ppermute | solution.py:23
  79.8 0.6 collective-permute-start.18
  81.5 4.1 %shard_map.148 = bf16[16,256,256]{2,1,0:T(8,128)(2,1)} custom-call(bf16[16,256,256]{2,1,0:T(8,128)(2,1)} %get-tuple-element.126.keep, bf16[16,256,256]{2,1,0:T(8,128)(2,1)} %collective-permute-done.16.got), custom_call_target="tpu_custom_call" | custom-call | flops 1000 | bytes 1000 | tf_op jit(solution)/shard_map/pallas_call | solution.py:307
  85.5 6.9 %all-to-all-start.1 = ((bf16[16,256,256]{2,1,0:T(8,128)(2,1)}), bf16[16,256,256]{2,1,0:T(8,128)(2,1)}, u32[]{:S(2)}, u32[]{:S(2)}) async-start(bf16[16,256,256]{2,1,0:T(8,128)(2,1)} %shard_map.148), calls=%async_computation.1 | async-start | bytes 4194304 | tf_op jit(solution)/shard_map/all_to_all | solution.py:538
  92.5 3.9 %shard_map.149 = (bf16[128,1024]{1,0:T(8,128)(2,1)}, bf16[128,1024]{1,0:T(8,128)(2,1)}, bf16[128,1024]{1,0:T(8,128)(2,1)}, bf16[128,1024]{1,0:T(8,128)(2,1)}) custom-call(bf16[512,1024]{1,0:T(8,128)(2,1)} %get-tuple-element.124.refs_9_.refs_0_, bf16[256,1024]{1,0:T(8,128)(2,1)} %refs_1_.1, bf16[256,1024]{1,0:T(8,128)(2,1)} %copy-done.7, ...), custom_call_target="tpu_custom_call" | custom-call | flops 1000 | bytes 1000 | tf_op jit(solution)/shard_map/pallas_call | solution.py:337
  97.1 1.3 collective-permute-start.20
  98.3 2.2 %collective-permute-start.21 = (bf16[128,1024]{1,0:T(8,128)(2,1)S(1)}, bf16[128,1024]{1,0:T(8,128)(2,1)S(1)}, u32[]{:S(2)}, u32[]{:S(2)}) collective-permute-start(bf16[128,1024]{1,0:T(8,128)(2,1)S(1)} %fusion.8.coarse_grad.right0), channel_id=1, source_target_pairs={{0,8},{4,12},{8,0},{12,4},{1,9},{5,13},{9,1},{13,5},{2,10},{6,14},... | collective-permute-start | bytes 786440 | tf_op jit(solution)/shard_map/ppermute | solution.py:23
  100.6 1.2 collective-permute-start.22
  101.8 6.0 %shard_map.150 = (bf16[16,32,512]{2,1,0:T(8,128)(2,1)}, bf16[2,8,16,256]{3,2,1,0:T(8,128)(2,1)}, bf16[2,8,16,256]{3,2,1,0:T(8,128)(2,1)}, bf16[2,8,16,256]{3,2,1,0:T(8,128)(2,1)}, bf16[2,8,16,256]{3,2,1,0:T(8,128)(2,1)}) custom-call(s32[7]{0:T(128)} %stack.42.place_ref.refs_0_.place, bf16[128,1024]{1,0:T(8,128)(2,1)} %copy-done.3, f32[1,2048]{1,0:T(1,128)} %bitcast.31, ...), custom_call_target="tpu_custom_call" | custom-call | flops 1000 | bytes 1000 | tf_op jit(solution)/shard_map/pallas_call | solution.py:469
  108.1 0.9 collective-permute-start.25
  109.0 1.6 collective-permute-start.26
  110.5 1.4 collective-permute-done.21.right2
  112.0 0.7 copy-done.21
  112.8 3.2 %shard_map.151 = (bf16[16,16,1024]{2,1,0:T(8,128)(2,1)}, bf16[16,16,1024]{2,1,0:T(8,128)(2,1)}) custom-call(s32[7]{0:T(128)} %stack.42.place_ref.refs_0_.place, bf16[4,128,512]{2,1,0:T(8,128)(2,1)} %copy-done.5, bf16[128,1024]{1,0:T(8,128)(2,1)} %copy-done.3, bf16[128,1024]{1,0:T(8,128)(2,1)} %copy-done.20, bf16[128,1024]{1,0:T(8,128)(2,1)} %copy-done.21, ...), custom_call_target="tpu_custom_call" | custom-call | flops 1000 | bytes 1000 | tf_op jit(solution)/shard_map/pallas_call | solution.py:362
  116.0 2.6 %collective-permute-start.23 = (bf16[16,16,1024]{2,1,0:T(8,128)(2,1)}, bf16[16,16,1024]{2,1,0:T(8,128)(2,1)S(1)}, u32[]{:S(2)}, u32[]{:S(2)}) collective-permute-start(bf16[16,16,1024]{2,1,0:T(8,128)(2,1)} %get-tuple-element.149), channel_id=1, source_target_pairs={{0,1},{1,0},{2,3},{3,2},{4,5},{5,4},{6,7},{7,6},{8,9},{9,8},{10,11... | collective-permute-start | bytes 1572872 | tf_op jit(solution)/shard_map/ppermute | solution.py:23
  118.6 1.0 add_convert_fusion
  119.6 0.6 slice_bitcast_fusion
  120.7 0.9 collective-permute-done.27.proj_got
  121.6 0.6 copy-done.28
  122.4 2.2 %shard_map.152 = bf16[16,80,256]{2,1,0:T(8,128)(2,1)} custom-call(bf16[16,16,1024]{2,1,0:T(8,128)(2,1)} %get-tuple-element.148.merge_keep, bf16[16,16,1024]{2,1,0:T(8,128)(2,1)} %copy-done.17, bf16[8,16,256]{2,1,0:T(8,128)(2,1)} %get-tuple-element.188.proj_keep, bf16[8,16,256]{2,1,0:T(8,128)(2,1)} %copy-done.28), custom_call_target="tpu_custom_call" | custom-call | flops 1000 | bytes 1000 | tf_op jit(solution)/shard_map/pallas_call | solution.py:307
  124.6 19.5 %all_to_all.20.merges = bf16[16,80,256]{2,1,0:T(8,128)(2,1)} all-to-all(bf16[16,80,256]{2,1,0:T(8,128)(2,1)} %shard_map.152), channel_id=1, replica_groups=mesh['xh'=2,'z'=4,'y'=4,'xl'=2,'c'=2] {'xh','z','xl'}, dimensions={0} | all-to-all | bytes 1310720 | tf_op jit(solution)/shard_map/all_to_all | solution.py:556
  144.1 3.2 %shard_map.153 = (bf16[8,272,256]{2,1,0:T(8,128)(2,1)}, f32[16,1024]{1,0:T(8,128)}) custom-call(bf16[16,256,256]{2,1,0:T(8,128)(2,1)} %all-to-all-done.1.blocks, bf16[16,80,256]{2,1,0:T(8,128)(2,1)} %all_to_all.20.merges), custom_call_target="tpu_custom_call" | custom-call | flops 1000 | bytes 1000 | tf_op jit(solution)/shard_map/pallas_call | solution.py:307
  147.3 3.7 %all-to-all-start.3 = ((bf16[8,272,256]{2,1,0:T(8,128)(2,1)}), bf16[8,272,256]{2,1,0:T(8,128)(2,1)S(1)}, u32[]{:S(2)}, u32[]{:S(2)}) async-start(bf16[8,272,256]{2,1,0:T(8,128)(2,1)} %get-tuple-element.165), calls=%async_computation.3 | async-start | bytes 2228224 | tf_op jit(solution)/shard_map/all_to_all | solution.py:560
  151.0 1.7 collective-permute-start.28
  152.7 1.9 %collective-permute-start.29 = (bf16[128,1024]{1,0:T(8,128)(2,1)S(1)}, bf16[128,1024]{1,0:T(8,128)(2,1)S(1)}, u32[]{:S(2)}, u32[]{:S(2)}) collective-permute-start(bf16[128,1024]{1,0:T(8,128)(2,1)S(1)} %copy-done.31), channel_id=1, source_target_pairs={{0,8},{4,12},{8,0},{12,4},{1,9},{5,13},{9,1},{13,5},{2,10},{6,14},... | collective-permute-start | bytes 786440 | tf_op jit(solution)/shard_map/ppermute | solution.py:23
  154.6 3.5 %collective-permute-done.28 = bf16[128,1024]{1,0:T(8,128)(2,1)S(1)} collective-permute-done((bf16[128,1024]{1,0:T(8,128)(2,1)S(1)}, bf16[128,1024]{1,0:T(8,128)(2,1)S(1)}, u32[]{:S(2)}, u32[]{:S(2)}) %collective-permute-start.28) | collective-permute-done | bytes 262176 | tf_op jit(solution)/shard_map/ppermute | solution.py:23
  158.1 2.0 %collective-permute-done.29 = bf16[128,1024]{1,0:T(8,128)(2,1)S(1)} collective-permute-done((bf16[128,1024]{1,0:T(8,128)(2,1)S(1)}, bf16[128,1024]{1,0:T(8,128)(2,1)S(1)}, u32[]{:S(2)}, u32[]{:S(2)}) %collective-permute-start.29) | collective-permute-done | bytes 262176 | tf_op jit(solution)/shard_map/ppermute | solution.py:23
  160.1 7.6 %collective-permute-done.30 = bf16[128,1024]{1,0:T(8,128)(2,1)S(1)} collective-permute-done((bf16[128,1024]{1,0:T(8,128)(2,1)S(1)}, bf16[128,1024]{1,0:T(8,128)(2,1)S(1)}, u32[]{:S(2)}, u32[]{:S(2)}) %collective-permute-start.30) | collective-permute-done | bytes 262176 | tf_op jit(solution)/shard_map/ppermute | solution.py:23
  167.7 0.9 fusion.10
  168.7 1.4 collective-permute-start.32
  170.1 2.0 %collective-permute-start.33 = (bf16[8,16,256]{2,1,0:T(8,128)(2,1)S(1)}, bf16[8,16,256]{2,1,0:T(8,128)(2,1)S(1)}, u32[]{:S(2)}, u32[]{:S(2)}) collective-permute-start(bf16[8,16,256]{2,1,0:T(8,128)(2,1)S(1)} %get-tuple-element.182), channel_id=1, source_target_pairs={{0,12},{4,0},{8,4},{12,8},{1,13},{5,1},{9,5},{13,9},{2,14},{6,2},{... | collective-permute-start | bytes 196616 | tf_op jit(solution)/shard_map/ppermute | solution.py:23
  172.1 2.7 %shard_map.154 = (f32[1024,256]{1,0:T(8,128)}, f32[256,1024]{1,0:T(8,128)}) custom-call(bf16[8,272,256]{2,1,0:T(8,128)(2,1)} %copy-done.1), custom_call_target="tpu_custom_call" | custom-call | flops 1000 | bytes 1000 | tf_op jit(solution)/shard_map/pallas_call | solution.py:386
  174.9 1.9 %collective-permute-start.34 = (bf16[4,8,16,256]{3,2,1,0:T(8,128)(2,1)S(1)}, bf16[4,8,16,256]{3,2,1,0:T(8,128)(2,1)S(1)}, u32[]{:S(2)}, u32[]{:S(2)}) collective-permute-start(bf16[4,8,16,256]{3,2,1,0:T(8,128)(2,1)S(1)} %pad_maximum_fusion.own), channel_id=1, source_target_pairs={{0,1},{1,0},{2,3},{3,2},{4,5},{5,4},{6,7},{7,6},{8,9},{9,8},{10,11... | collective-permute-start | bytes 786440 | tf_op jit(solution)/shard_map/ppermute | solution.py:23
  176.8 1.2 collective-permute-done.34.other
  178.0 0.7 copy-done.23
  178.7 2.1 %shard_map.155 = f32[512,512]{1,0:T(8,128)} custom-call(s32[7]{0:T(128)} %stack.42.place_ref.refs_0_.place, bf16[4,8,16,256]{3,2,1,0:T(8,128)(2,1)} %copy-done.14, bf16[4,8,16,256]{3,2,1,0:T(8,128)(2,1)} %copy-done.23), custom_call_target="tpu_custom_call" | custom-call | flops 1000 | bytes 1000 | tf_op jit(solution)/shard_map/pallas_call | solution.py:412
  (111 shorter events, 5.5 us)
Async XLA Ops:
  1.6 10.3 %collective-permute-start = (bf16[4,32,512]{2,1,0:T(8,128)(2,1)S(1)}, bf16[4,32,512]{2,1,0:T(8,128)(2,1)S(1)}, u32[]{:S(2)}, u32[]{:S(2)}) collective-permute-start(bf16[4,32,512]{2,1,0:T(8,128)(2,1)S(1)} %get-tuple-element.186), channel_id=1, source_target_pairs={{0,16},{16,32},{32,48},{48,64},{64,80},{80,96},{96,112},{112,0},{1... | collective-permute-start | bytes 393224 | tf_op jit(solution)/shard_map/ppermute | solution.py:23
  4.2 7.8 %collective-permute-start.1 = (bf16[4,32,512]{2,1,0:T(8,128)(2,1)S(1)}, bf16[4,32,512]{2,1,0:T(8,128)(2,1)S(1)}, u32[]{:S(2)}, u32[]{:S(2)}) collective-permute-start(bf16[4,32,512]{2,1,0:T(8,128)(2,1)S(1)} %get-tuple-element.185), channel_id=1, source_target_pairs={{0,112},{16,0},{32,16},{48,32},{64,48},{80,64},{96,80},{112,96},{1... | collective-permute-start | bytes 393224 | tf_op jit(solution)/shard_map/ppermute | solution.py:23
  12.0 13.0 %copy-start.24 = (bf16[4,32,512]{2,1,0:T(8,128)(2,1)}, bf16[4,32,512]{2,1,0:T(8,128)(2,1)S(1)}, u32[]{:S(2)}) copy-start(bf16[4,32,512]{2,1,0:T(8,128)(2,1)S(1)} %collective-permute-done.top_ref) | copy-start | bytes 393220
  12.0 9.6 %copy-start.25 = (bf16[4,32,512]{2,1,0:T(8,128)(2,1)}, bf16[4,32,512]{2,1,0:T(8,128)(2,1)S(1)}, u32[]{:S(2)}) copy-start(bf16[4,32,512]{2,1,0:T(8,128)(2,1)S(1)} %collective-permute-done.1.bottom_ref) | copy-start | bytes 393220
  12.1 4.1 %collective-permute-start.3 = (bf16[24,4,512]{2,1,0:T(4,128)(2,1)S(1)}, bf16[24,4,512]{2,1,0:T(4,128)(2,1)S(1)}, u32[]{:S(2)}, u32[]{:S(2)}) collective-permute-start(bf16[24,4,512]{2,1,0:T(4,128)(2,1)S(1)} %pad_maximum_fusion.2), channel_id=1, source_target_pairs={{0,15},{1,0},{2,1},{3,2},{4,3},{5,4},{6,5},{7,6},{8,7},{9,8},{10,9... | collective-permute-start | bytes 294920 | tf_op jit(solution)/shard_map/ppermute | solution.py:23
  13.5 2.8 %collective-permute-start.2 = (bf16[24,4,512]{2,1,0:T(4,128)(2,1)S(1)}, bf16[24,4,512]{2,1,0:T(4,128)(2,1)S(1)}, u32[]{:S(2)}, u32[]{:S(2)}) collective-permute-start(bf16[24,4,512]{2,1,0:T(4,128)(2,1)S(1)} %pad_maximum_fusion.1), channel_id=1, source_target_pairs={{0,1},{1,2},{2,3},{3,4},{4,5},{5,6},{6,7},{7,8},{8,9},{9,10},{10,1... | collective-permute-start | bytes 294920 | tf_op jit(solution)/shard_map/ppermute | solution.py:23
  16.2 6.8 %copy-start.26 = (bf16[24,4,512]{2,1,0:T(4,128)(2,1)}, bf16[24,4,512]{2,1,0:T(4,128)(2,1)S(1)}, u32[]{:S(2)}) copy-start(bf16[24,4,512]{2,1,0:T(4,128)(2,1)S(1)} %collective-permute-done.3.right_ref) | copy-start | bytes 294916
  16.2 8.1 %copy-start.27 = (bf16[24,4,512]{2,1,0:T(4,128)(2,1)}, bf16[24,4,512]{2,1,0:T(4,128)(2,1)S(1)}, u32[]{:S(2)}) copy-start(bf16[24,4,512]{2,1,0:T(4,128)(2,1)S(1)} %collective-permute-done.2.left_ref) | copy-start | bytes 294916
  16.2 20.6 %collective-permute-start.4 = (bf16[1024,256]{1,0:T(8,128)(2,1)}, bf16[1024,256]{1,0:T(8,128)(2,1)}, u32[]{:S(2)}, u32[]{:S(2)}) collective-permute-start(bf16[1024,256]{1,0:T(8,128)(2,1)} %refs_8_.1), channel_id=1, source_target_pairs={{0,2},{2,0},{1,3},{3,1},{4,6},{6,4},{5,7},{7,5},{8,10},{10,8},{9,1... | collective-permute-start | bytes 1572872 | tf_op jit(solution)/shard_map/ppermute | solution.py:23
  18.8 18.0 %collective-permute-start.5 = (bf16[1024,256]{1,0:T(8,128)(2,1)}, bf16[1024,256]{1,0:T(8,128)(2,1)S(1)}, u32[]{:S(2)}, u32[]{:S(2)}) collective-permute-start(bf16[1024,256]{1,0:T(8,128)(2,1)} %refs_8_.1), channel_id=1, source_target_pairs={{0,1},{1,0},{2,3},{3,2},{4,5},{5,4},{6,7},{7,6},{8,9},{9,8},{10,11... | collective-permute-start | bytes 1572872 | tf_op jit(solution)/shard_map/ppermute | solution.py:23
  21.6 14.9 %collective-permute-start.6 = (bf16[128,1024]{1,0:T(8,128)(2,1)}, bf16[128,1024]{1,0:T(8,128)(2,1)S(1)}, u32[]{:S(2)}, u32[]{:S(2)}) collective-permute-start(bf16[128,1024]{1,0:T(8,128)(2,1)} %bitcast.20), channel_id=1, source_target_pairs={{0,4},{4,8},{8,12},{12,0},{1,5},{5,9},{9,13},{13,1},{2,6},{6,10},{... | collective-permute-start | bytes 786440 | tf_op jit(solution)/shard_map/ppermute | solution.py:23
  21.6 14.9 %collective-permute-start.7 = (bf16[128,1024]{1,0:T(8,128)(2,1)}, bf16[128,1024]{1,0:T(8,128)(2,1)S(1)}, u32[]{:S(2)}, u32[]{:S(2)}) collective-permute-start(bf16[128,1024]{1,0:T(8,128)(2,1)} %bitcast.21), channel_id=1, source_target_pairs={{0,8},{4,12},{8,0},{12,4},{1,9},{5,13},{9,1},{13,5},{2,10},{6,14},... | collective-permute-start | bytes 786440 | tf_op jit(solution)/shard_map/ppermute | solution.py:23
  23.0 13.8 %collective-permute-start.8 = (bf16[128,1024]{1,0:T(8,128)(2,1)}, bf16[128,1024]{1,0:T(8,128)(2,1)S(1)}, u32[]{:S(2)}, u32[]{:S(2)}) collective-permute-start(bf16[128,1024]{1,0:T(8,128)(2,1)} %bitcast.22), channel_id=1, source_target_pairs={{0,12},{4,0},{8,4},{12,8},{1,13},{5,1},{9,5},{13,9},{2,14},{6,2},{... | collective-permute-start | bytes 786440 | tf_op jit(solution)/shard_map/ppermute | solution.py:23
  24.9 13.7 %copy-start.4 = (bf16[256,1024]{1,0:T(8,128)(2,1)S(1)}, bf16[256,1024]{1,0:T(8,128)(2,1)}, u32[]{:S(2)}) copy-start(bf16[256,1024]{1,0:T(8,128)(2,1)} %refs_1_.1) | copy-start | bytes 1572868
  36.5 25.4 %copy-start.8 = (bf16[128,1024]{1,0:T(8,128)(2,1)}, bf16[128,1024]{1,0:T(8,128)(2,1)S(1)}, u32[]{:S(2)}) copy-start(bf16[128,1024]{1,0:T(8,128)(2,1)S(1)} %collective-permute-done.6.refs_5_.refs_6_) | copy-start | bytes 786436
  36.8 1.9 %copy-start.15 = (bf16[1024,256]{1,0:T(8,128)(2,1)}, bf16[1024,256]{1,0:T(8,128)(2,1)S(1)}, u32[]{:S(2)}) copy-start(bf16[1024,256]{1,0:T(8,128)(2,1)S(1)} %collective-permute-done.5.refs_9_) | copy-start | bytes 1572868
  37.5 18.5 %collective-permute-start.12 = (bf16[1024,256]{1,0:T(8,128)(2,1)}, bf16[1024,256]{1,0:T(8,128)(2,1)S(1)}, u32[]{:S(2)}, u32[]{:S(2)}) collective-permute-start(bf16[1024,256]{1,0:T(8,128)(2,1)} %collective-permute-done.4.refs_10_), channel_id=1, source_target_pairs={{0,1},{1,0},{2,3},{3,2},{4,5},{5,4},{6,7},{7,6},{8,9},{9,8},{10,11... | collective-permute-start | bytes 1572872 | tf_op jit(solution)/shard_map/ppermute | solution.py:23
  38.7 17.3 %collective-permute-start.13 = (bf16[256,1024]{1,0:T(8,128)(2,1)S(1)}, bf16[256,1024]{1,0:T(8,128)(2,1)S(1)}, u32[]{:S(2)}, u32[]{:S(2)}) collective-permute-start(bf16[256,1024]{1,0:T(8,128)(2,1)S(1)} %copy-done.4), channel_id=1, source_target_pairs={{0,2},{2,0},{1,3},{3,1},{4,6},{6,4},{5,7},{7,5},{8,10},{10,8},{9,1... | collective-permute-start | bytes 1572872 | tf_op jit(solution)/shard_map/ppermute | solution.py:23
  40.4 9.2 %collective-permute-start.10 = (bf16[128,1024]{1,0:T(8,128)(2,1)}, bf16[128,1024]{1,0:T(8,128)(2,1)S(1)}, u32[]{:S(2)}, u32[]{:S(2)}) collective-permute-start(bf16[128,1024]{1,0:T(8,128)(2,1)} %get-tuple-element.105.refs_0_.refs_1_), channel_id=1, source_target_pairs={{0,8},{4,12},{8,0},{12,4},{1,9},{5,13},{9,1},{13,5},{2,10},{6,14},... | collective-permute-start | bytes 786440 | tf_op jit(solution)/shard_map/ppermute | solution.py:23
  41.1 13.9 %collective-permute-start.11 = (bf16[128,1024]{1,0:T(8,128)(2,1)}, bf16[128,1024]{1,0:T(8,128)(2,1)S(1)}, u32[]{:S(2)}, u32[]{:S(2)}) collective-permute-start(bf16[128,1024]{1,0:T(8,128)(2,1)} %get-tuple-element.105.refs_0_.refs_1_), channel_id=1, source_target_pairs={{0,12},{4,0},{8,4},{12,8},{1,13},{5,1},{9,5},{13,9},{2,14},{6,2},{... | collective-permute-start | bytes 786440 | tf_op jit(solution)/shard_map/ppermute | solution.py:23
  42.8 13.2 %collective-permute-start.9 = (bf16[128,1024]{1,0:T(8,128)(2,1)}, bf16[128,1024]{1,0:T(8,128)(2,1)S(1)}, u32[]{:S(2)}, u32[]{:S(2)}) collective-permute-start(bf16[128,1024]{1,0:T(8,128)(2,1)} %get-tuple-element.105.refs_0_.refs_1_), channel_id=1, source_target_pairs={{0,4},{4,8},{8,12},{12,0},{1,5},{5,9},{9,13},{13,1},{2,6},{6,10},{... | collective-permute-start | bytes 786440 | tf_op jit(solution)/shard_map/ppermute | solution.py:23
  49.6 7.8 %copy-start.11 = (bf16[128,1024]{1,0:T(8,128)(2,1)}, bf16[128,1024]{1,0:T(8,128)(2,1)S(1)}, u32[]{:S(2)}) copy-start(bf16[128,1024]{1,0:T(8,128)(2,1)S(1)} %collective-permute-done.10.refs_2_.refs_3_) | copy-start | bytes 786436
  54.9 2.4 %copy-start.12 = (bf16[128,1024]{1,0:T(8,128)(2,1)}, bf16[128,1024]{1,0:T(8,128)(2,1)S(1)}, u32[]{:S(2)}) copy-start(bf16[128,1024]{1,0:T(8,128)(2,1)S(1)} %collective-permute-done.11.refs_3_.refs_4_) | copy-start | bytes 786436
  56.0 0.9 copy-start.16
  56.0 5.9 %copy-start.6 = (bf16[256,1024]{1,0:T(8,128)(2,1)}, bf16[256,1024]{1,0:T(8,128)(2,1)S(1)}, u32[]{:S(2)}) copy-start(bf16[256,1024]{1,0:T(8,128)(2,1)S(1)} %collective-permute-done.13.refs_14_.refs_3_) | copy-start | bytes 1572868
  56.0 5.0 %collective-permute-start.14 = (bf16[256,1024]{1,0:T(8,128)(2,1)S(1)}, bf16[256,1024]{1,0:T(8,128)(2,1)S(1)}, u32[]{:S(2)}, u32[]{:S(2)}) collective-permute-start(bf16[256,1024]{1,0:T(8,128)(2,1)S(1)} %copy-done.4), channel_id=1, source_target_pairs={{0,1},{1,0},{2,3},{3,2},{4,5},{5,4},{6,7},{7,6},{8,9},{9,8},{10,11... | collective-permute-start | bytes 1572872 | tf_op jit(solution)/shard_map/ppermute | solution.py:23
  56.9 5.0 %collective-permute-start.15 = (bf16[256,1024]{1,0:T(8,128)(2,1)S(1)}, bf16[256,1024]{1,0:T(8,128)(2,1)}, u32[]{:S(2)}, u32[]{:S(2)}) collective-permute-start(bf16[256,1024]{1,0:T(8,128)(2,1)S(1)} %collective-permute-done.13.refs_14_.refs_3_), channel_id=1, source_target_pairs={{0,1},{1,0},{2,3},{3,2},{4,5},{5,4},{6,7},{7,6},{8,9},{9,8},{10,11... | collective-permute-start | bytes 1572872 | tf_op jit(solution)/shard_map/ppermute | solution.py:23
  57.4 13.1 %all-to-all-start = ((bf16[4,128,512]{2,1,0:T(8,128)(2,1)}), bf16[4,128,512]{2,1,0:T(8,128)(2,1)S(1)}, u32[]{:S(2)}, u32[]{:S(2)}) async-start(bf16[4,128,512]{2,1,0:T(8,128)(2,1)} %get-tuple-element.123), calls=%async_computation | async-start | bytes 1048576 | tf_op jit(solution)/shard_map/all_to_all | solution.py:523
  61.0 0.8 copy-start.7
  70.5 6.1 %copy-start.5 = (bf16[4,128,512]{2,1,0:T(8,128)(2,1)}, bf16[4,128,512]{2,1,0:T(8,128)(2,1)S(1)}, u32[]{:S(2)}) copy-start(bf16[4,128,512]{2,1,0:T(8,128)(2,1)S(1)} %all-to-all-done.left) | copy-start | bytes 1572868
  70.5 6.9 %copy-start = (bf16[128,1024]{1,0:T(8,128)(2,1)S(1)}, bf16[128,1024]{1,0:T(8,128)(2,1)}, u32[]{:S(2)}) copy-start(bf16[128,1024]{1,0:T(8,128)(2,1)} %get-tuple-element.129) | copy-start | bytes 786436
  70.5 9.9 %copy-start.33 = (bf16[128,1024]{1,0:T(8,128)(2,1)S(1)}, bf16[128,1024]{1,0:T(8,128)(2,1)}, u32[]{:S(2)}) copy-start(bf16[128,1024]{1,0:T(8,128)(2,1)} %get-tuple-element.133) | copy-start | bytes 786436
  76.6 4.9 %collective-permute-start.16 = (bf16[16,256,256]{2,1,0:T(8,128)(2,1)}, bf16[16,256,256]{2,1,0:T(8,128)(2,1)}, u32[]{:S(2)}, u32[]{:S(2)}) collective-permute-start(bf16[16,256,256]{2,1,0:T(8,128)(2,1)} %get-tuple-element.127), channel_id=1, source_target_pairs={{0,1},{1,0},{2,3},{3,2},{4,5},{5,4},{6,7},{7,6},{8,9},{9,8},{10,11... | collective-permute-start | bytes 6291464 | tf_op jit(solution)/shard_map/ppermute | solution.py:23
  77.5 18.9 %collective-permute-start.17 = (bf16[128,1024]{1,0:T(8,128)(2,1)}, bf16[128,1024]{1,0:T(8,128)(2,1)S(1)}, u32[]{:S(2)}, u32[]{:S(2)}) collective-permute-start(bf16[128,1024]{1,0:T(8,128)(2,1)} %get-tuple-element.131), channel_id=1, source_target_pairs={{0,12},{4,0},{8,4},{12,8},{1,13},{5,1},{9,5},{13,9},{2,14},{6,2},{... | collective-permute-start | bytes 786440 | tf_op jit(solution)/shard_map/ppermute | solution.py:23
  79.8 16.6 %collective-permute-start.18 = (bf16[128,1024]{1,0:T(8,128)(2,1)}, bf16[128,1024]{1,0:T(8,128)(2,1)S(1)}, u32[]{:S(2)}, u32[]{:S(2)}) collective-permute-start(bf16[128,1024]{1,0:T(8,128)(2,1)} %get-tuple-element.132), channel_id=1, source_target_pairs={{0,8},{4,12},{8,0},{12,4},{1,9},{5,13},{9,1},{13,5},{2,10},{6,14},... | collective-permute-start | bytes 786440 | tf_op jit(solution)/shard_map/ppermute | solution.py:23
  80.4 16.0 %collective-permute-start.19 = (bf16[128,1024]{1,0:T(8,128)(2,1)S(1)}, bf16[128,1024]{1,0:T(8,128)(2,1)S(1)}, u32[]{:S(2)}, u32[]{:S(2)}) collective-permute-start(bf16[128,1024]{1,0:T(8,128)(2,1)S(1)} %copy-done.33), channel_id=1, source_target_pairs={{0,4},{4,8},{8,12},{12,0},{1,5},{5,9},{9,13},{13,1},{2,6},{6,10},{... | collective-permute-start | bytes 786440 | tf_op jit(solution)/shard_map/ppermute | solution.py:23
  85.5 39.1 %all-to-all-start.1 = ((bf16[16,256,256]{2,1,0:T(8,128)(2,1)}), bf16[16,256,256]{2,1,0:T(8,128)(2,1)}, u32[]{:S(2)}, u32[]{:S(2)}) async-start(bf16[16,256,256]{2,1,0:T(8,128)(2,1)} %shard_map.148), calls=%async_computation.1 | async-start | bytes 4194304 | tf_op jit(solution)/shard_map/all_to_all | solution.py:538
  92.5 3.9 %copy-start.19 = (bf16[128,1024]{1,0:T(8,128)(2,1)S(1)}, bf16[128,1024]{1,0:T(8,128)(2,1)}, u32[]{:S(2)}) copy-start(bf16[128,1024]{1,0:T(8,128)(2,1)} %get-tuple-element.130) | copy-start | bytes 786436
  92.5 3.9 %copy-start.29 = (f32[1024]{0:T(1024)S(1)}, f32[1024]{0:T(1024)}, u32[]{:S(2)}) copy-start(f32[1024]{0:T(1024)} %param.16) | copy-start | bytes 12292
  92.5 4.3 %copy-start.2 = (bf16[8,16,1024]{2,1,0:T(8,128)(2,1)S(1)}, bf16[8,16,1024]{2,1,0:T(8,128)(2,1)}, u32[]{:S(2)}) copy-start(bf16[8,16,1024]{2,1,0:T(8,128)(2,1)} %param.19) | copy-start | bytes 786436
  97.1 4.7 %copy-start.3 = (bf16[128,1024]{1,0:T(8,128)(2,1)}, bf16[128,1024]{1,0:T(8,128)(2,1)S(1)}, u32[]{:S(2)}) copy-start(bf16[128,1024]{1,0:T(8,128)(2,1)S(1)} %fusion.8.coarse_grad.right0) | copy-start | bytes 786436
  97.1 11.9 %collective-permute-start.20 = (bf16[128,1024]{1,0:T(8,128)(2,1)S(1)}, bf16[128,1024]{1,0:T(8,128)(2,1)S(1)}, u32[]{:S(2)}, u32[]{:S(2)}) collective-permute-start(bf16[128,1024]{1,0:T(8,128)(2,1)S(1)} %fusion.8.coarse_grad.right0), channel_id=1, source_target_pairs={{0,4},{4,8},{8,12},{12,0},{1,5},{5,9},{9,13},{13,1},{2,6},{6,10},{... | collective-permute-start | bytes 786440 | tf_op jit(solution)/shard_map/ppermute | solution.py:23
  98.3 13.7 %collective-permute-start.21 = (bf16[128,1024]{1,0:T(8,128)(2,1)S(1)}, bf16[128,1024]{1,0:T(8,128)(2,1)S(1)}, u32[]{:S(2)}, u32[]{:S(2)}) collective-permute-start(bf16[128,1024]{1,0:T(8,128)(2,1)S(1)} %fusion.8.coarse_grad.right0), channel_id=1, source_target_pairs={{0,8},{4,12},{8,0},{12,4},{1,9},{5,13},{9,1},{13,5},{2,10},{6,14},... | collective-permute-start | bytes 786440 | tf_op jit(solution)/shard_map/ppermute | solution.py:23
  100.6 11.4 %collective-permute-start.22 = (bf16[128,1024]{1,0:T(8,128)(2,1)S(1)}, bf16[128,1024]{1,0:T(8,128)(2,1)S(1)}, u32[]{:S(2)}, u32[]{:S(2)}) collective-permute-start(bf16[128,1024]{1,0:T(8,128)(2,1)S(1)} %fusion.8.coarse_grad.right0), channel_id=1, source_target_pairs={{0,12},{4,0},{8,4},{12,8},{1,13},{5,1},{9,5},{13,9},{2,14},{6,2},{... | collective-permute-start | bytes 786440 | tf_op jit(solution)/shard_map/ppermute | solution.py:23
  107.8 10.8 %collective-permute-start.24 = (bf16[2,8,16,256]{3,2,1,0:T(8,128)(2,1)}, bf16[2,8,16,256]{3,2,1,0:T(8,128)(2,1)S(1)}, u32[]{:S(2)}, u32[]{:S(2)}) collective-permute-start(bf16[2,8,16,256]{3,2,1,0:T(8,128)(2,1)} %get-tuple-element.151), channel_id=1, source_target_pairs={{0,4},{4,8},{8,12},{12,0},{1,5},{5,9},{9,13},{13,1},{2,6},{6,10},{... | collective-permute-start | bytes 393224 | tf_op jit(solution)/shard_map/ppermute | solution.py:23
  108.1 10.5 %collective-permute-start.25 = (bf16[2,8,16,256]{3,2,1,0:T(8,128)(2,1)}, bf16[2,8,16,256]{3,2,1,0:T(8,128)(2,1)S(1)}, u32[]{:S(2)}, u32[]{:S(2)}) collective-permute-start(bf16[2,8,16,256]{3,2,1,0:T(8,128)(2,1)} %get-tuple-element.152), channel_id=1, source_target_pairs={{0,8},{4,12},{8,0},{12,4},{1,9},{5,13},{9,1},{13,5},{2,10},{6,14},... | collective-permute-start | bytes 393224 | tf_op jit(solution)/shard_map/ppermute | solution.py:23
  109.0 3.0 %copy-start.20 = (bf16[128,1024]{1,0:T(8,128)(2,1)}, bf16[128,1024]{1,0:T(8,128)(2,1)S(1)}, u32[]{:S(2)}) copy-start(bf16[128,1024]{1,0:T(8,128)(2,1)S(1)} %collective-permute-done.20.right1) | copy-start | bytes 786436
  109.0 9.6 %collective-permute-start.26 = (bf16[2,8,16,256]{3,2,1,0:T(8,128)(2,1)}, bf16[2,8,16,256]{3,2,1,0:T(8,128)(2,1)S(1)}, u32[]{:S(2)}, u32[]{:S(2)}) collective-permute-start(bf16[2,8,16,256]{3,2,1,0:T(8,128)(2,1)} %get-tuple-element.153), channel_id=1, source_target_pairs={{0,12},{4,0},{8,4},{12,8},{1,13},{5,1},{9,5},{13,9},{2,14},{6,2},{... | collective-permute-start | bytes 393224 | tf_op jit(solution)/shard_map/ppermute | solution.py:23
  116.0 5.6 %collective-permute-start.23 = (bf16[16,16,1024]{2,1,0:T(8,128)(2,1)}, bf16[16,16,1024]{2,1,0:T(8,128)(2,1)S(1)}, u32[]{:S(2)}, u32[]{:S(2)}) collective-permute-start(bf16[16,16,1024]{2,1,0:T(8,128)(2,1)} %get-tuple-element.149), channel_id=1, source_target_pairs={{0,1},{1,0},{2,3},{3,2},{4,5},{5,4},{6,7},{7,6},{8,9},{9,8},{10,11... | collective-permute-start | bytes 1572872 | tf_op jit(solution)/shard_map/ppermute | solution.py:23
  120.2 1.4 collective-permute-start.27
  144.1 10.5 %copy-start.30 = (bf16[128,1024]{1,0:T(8,128)(2,1)S(1)}, bf16[128,1024]{1,0:T(8,128)(2,1)}, u32[]{:S(2)}) copy-start(bf16[128,1024]{1,0:T(8,128)(2,1)} %get-tuple-element.169) | copy-start | bytes 786436
  144.1 23.6 %copy-start.18 = (bf16[128,1024]{1,0:T(8,128)(2,1)S(1)}, bf16[128,1024]{1,0:T(8,128)(2,1)}, u32[]{:S(2)}) copy-start(bf16[128,1024]{1,0:T(8,128)(2,1)} %get-tuple-element.166) | copy-start | bytes 786436
  147.3 3.7 %copy-start.32 = (bf16[128,1024]{1,0:T(8,128)(2,1)S(1)}, bf16[128,1024]{1,0:T(8,128)(2,1)}, u32[]{:S(2)}) copy-start(bf16[128,1024]{1,0:T(8,128)(2,1)} %get-tuple-element.167) | copy-start | bytes 786436
  147.3 5.4 %copy-start.31 = (bf16[128,1024]{1,0:T(8,128)(2,1)S(1)}, bf16[128,1024]{1,0:T(8,128)(2,1)}, u32[]{:S(2)}) copy-start(bf16[128,1024]{1,0:T(8,128)(2,1)} %get-tuple-element.168) | copy-start | bytes 786436
  147.3 21.4 %all-to-all-start.3 = ((bf16[8,272,256]{2,1,0:T(8,128)(2,1)}), bf16[8,272,256]{2,1,0:T(8,128)(2,1)S(1)}, u32[]{:S(2)}, u32[]{:S(2)}) async-start(bf16[8,272,256]{2,1,0:T(8,128)(2,1)} %get-tuple-element.165), calls=%async_computation.3 | async-start | bytes 2228224 | tf_op jit(solution)/shard_map/all_to_all | solution.py:560
  151.0 7.1 %collective-permute-start.28 = (bf16[128,1024]{1,0:T(8,128)(2,1)S(1)}, bf16[128,1024]{1,0:T(8,128)(2,1)S(1)}, u32[]{:S(2)}, u32[]{:S(2)}) collective-permute-start(bf16[128,1024]{1,0:T(8,128)(2,1)S(1)} %copy-done.32), channel_id=1, source_target_pairs={{0,12},{4,0},{8,4},{12,8},{1,13},{5,1},{9,5},{13,9},{2,14},{6,2},{... | collective-permute-start | bytes 786440 | tf_op jit(solution)/shard_map/ppermute | solution.py:23
  152.7 7.4 %collective-permute-start.29 = (bf16[128,1024]{1,0:T(8,128)(2,1)S(1)}, bf16[128,1024]{1,0:T(8,128)(2,1)S(1)}, u32[]{:S(2)}, u32[]{:S(2)}) collective-permute-start(bf16[128,1024]{1,0:T(8,128)(2,1)S(1)} %copy-done.31), channel_id=1, source_target_pairs={{0,8},{4,12},{8,0},{12,4},{1,9},{5,13},{9,1},{13,5},{2,10},{6,14},... | collective-permute-start | bytes 786440 | tf_op jit(solution)/shard_map/ppermute | solution.py:23
  154.6 13.1 %collective-permute-start.30 = (bf16[128,1024]{1,0:T(8,128)(2,1)S(1)}, bf16[128,1024]{1,0:T(8,128)(2,1)S(1)}, u32[]{:S(2)}, u32[]{:S(2)}) collective-permute-start(bf16[128,1024]{1,0:T(8,128)(2,1)S(1)} %copy-done.30), channel_id=1, source_target_pairs={{0,4},{4,8},{8,12},{12,0},{1,5},{5,9},{9,13},{13,1},{2,6},{6,10},{... | collective-permute-start | bytes 786440 | tf_op jit(solution)/shard_map/ppermute | solution.py:23
  168.6 3.5 %copy-start.1 = (bf16[8,272,256]{2,1,0:T(8,128)(2,1)}, bf16[8,272,256]{2,1,0:T(8,128)(2,1)S(1)}, u32[]{:S(2)}) copy-start(bf16[8,272,256]{2,1,0:T(8,128)(2,1)S(1)} %all-to-all-done.3.blocks) | copy-start | bytes 3342340
  168.7 6.2 %collective-permute-start.31 = (bf16[8,16,256]{2,1,0:T(8,128)(2,1)S(1)}, bf16[8,16,256]{2,1,0:T(8,128)(2,1)S(1)}, u32[]{:S(2)}, u32[]{:S(2)}) collective-permute-start(bf16[8,16,256]{2,1,0:T(8,128)(2,1)S(1)} %get-tuple-element.182), channel_id=1, source_target_pairs={{0,4},{4,8},{8,12},{12,0},{1,5},{5,9},{9,13},{13,1},{2,6},{6,10},{... | collective-permute-start | bytes 196616 | tf_op jit(solution)/shard_map/ppermute | solution.py:23
  168.7 6.1 %collective-permute-start.32 = (bf16[8,16,256]{2,1,0:T(8,128)(2,1)S(1)}, bf16[8,16,256]{2,1,0:T(8,128)(2,1)S(1)}, u32[]{:S(2)}, u32[]{:S(2)}) collective-permute-start(bf16[8,16,256]{2,1,0:T(8,128)(2,1)S(1)} %get-tuple-element.182), channel_id=1, source_target_pairs={{0,8},{4,12},{8,0},{12,4},{1,9},{5,13},{9,1},{13,5},{2,10},{6,14},... | collective-permute-start | bytes 196616 | tf_op jit(solution)/shard_map/ppermute | solution.py:23
  170.1 4.7 %collective-permute-start.33 = (bf16[8,16,256]{2,1,0:T(8,128)(2,1)S(1)}, bf16[8,16,256]{2,1,0:T(8,128)(2,1)S(1)}, u32[]{:S(2)}, u32[]{:S(2)}) collective-permute-start(bf16[8,16,256]{2,1,0:T(8,128)(2,1)S(1)} %get-tuple-element.182), channel_id=1, source_target_pairs={{0,12},{4,0},{8,4},{12,8},{1,13},{5,1},{9,5},{13,9},{2,14},{6,2},{... | collective-permute-start | bytes 196616 | tf_op jit(solution)/shard_map/ppermute | solution.py:23
  174.9 3.1 %copy-start.14 = (bf16[4,8,16,256]{3,2,1,0:T(8,128)(2,1)}, bf16[4,8,16,256]{3,2,1,0:T(8,128)(2,1)S(1)}, u32[]{:S(2)}) copy-start(bf16[4,8,16,256]{3,2,1,0:T(8,128)(2,1)S(1)} %pad_maximum_fusion.own) | copy-start | bytes 786436
  174.9 3.1 %collective-permute-start.34 = (bf16[4,8,16,256]{3,2,1,0:T(8,128)(2,1)S(1)}, bf16[4,8,16,256]{3,2,1,0:T(8,128)(2,1)S(1)}, u32[]{:S(2)}, u32[]{:S(2)}) collective-permute-start(bf16[4,8,16,256]{3,2,1,0:T(8,128)(2,1)S(1)} %pad_maximum_fusion.own), channel_id=1, source_target_pairs={{0,1},{1,0},{2,3},{3,2},{4,5},{5,4},{6,7},{7,6},{8,9},{9,8},{10,11... | collective-permute-start | bytes 786440 | tf_op jit(solution)/shard_map/ppermute | solution.py:23
  (8 other events, 5.8 us)

commit v2 on v1

--- a/solution.py
+++ b/solution.py
@@ -280,18 +280,22 @@
     out[...] = add(keep[...], got[...])
 
 
-def all_sum_kernel(blocks, merges, out, merge_out):
+def block_sum_kernel(blocks, out):
     total = blocks[0].astype(F32)
-    merge = merges[0].astype(F32)
     for n in range(1, blocks.shape[0]):
         total += blocks[n].astype(F32)
+    out[...] = total.astype(BF)
+
+
+def all_sum_kernel(total, merges, out, merge_out):
+    merge = merges[0].astype(F32)
+    for n in range(1, merges.shape[0]):
         merge += merges[n].astype(F32)
     for n in range(4):
         merge_out[:, n * 256 : (n + 1) * 256] = merge[n * 16 : (n + 1) * 16, :]
-    total = total.astype(BF)
     proj = merge[64:, :].astype(BF)
     for n in range(out.shape[0]):
-        out[n, :256, :] = total
+        out[n, :256, :] = total[...]
         out[n, 256:, :] = proj
 
 
@@ -554,9 +558,10 @@
     blocks, merges, outer = together(blocks, merges, outer)
 
     merges = lax.all_to_all(merges, LAT + ("xl",), 0, 0)
-    merges, outer = together(merges, outer)
-
-    blocks, grad_merge = sums(all_sum_kernel, [(8, 272, 256), (16, 1024)], blocks, merges)
+    (total,) = sums(block_sum_kernel, [(256, 256)], blocks)
+    merges, outer, total = together(merges, outer, total)
+
+    blocks, grad_merge = sums(all_sum_kernel, [(8, 272, 256), (16, 1024)], total, merges)
     blocks = lax.all_to_all(blocks, LAT, 0, 0)
     summed = scatter_rel(outer, "y", -1)
     level_two = (coarse.astype(F32) + summed).astype(BF)

time: 181 us -> 182 us (level)
  blocking collectives: 19.5 us -> 0 us
  waiting for transfers between devices: 35.7 us -> 46.6 us
  starting transfers between devices: 61.9 us -> 68.5 us
    all_to_all x1 -> x0, blocking collectives: 19.5 us -> none  [per_device(): merges = lax.all_to_all(merges, LAT + ('xl',), 0, 0)]
    all_to_all x0 -> x1, waiting for transfers between devices: none -> 9.65 us  [per_device(): merges = lax.all_to_all(merges, LAT + ('xl',), 0, 0)]
    all_to_all x0 -> x1, starting transfers between devices: none -> 6.88 us  [per_device(): merges = lax.all_to_all(merges, LAT + ('xl',), 0, 0)]
    pallas_call x3 -> x4, Pallas kernels: 9.4 us -> 11.1 us  [sums(): pl.pallas_call(kernel, out_shape=[jax.ShapeDtypeStruct(shape, F32 if shap...]
    unnamed x68 -> x66, local copies, waits for them, and re-layouts: 4.2 us -> 5.03 us
  transfers between devices with their start and end apart: 38 -> 39, of which waited for: 14 -> 16; matrix products, arithmetic and copies ran while one was open for 3% -> 3% of each run, Pallas kernels for 23% -> 24%
where the time goes in v2:
time: 182 us; the launch traced here: 181 us
  starting transfers between devices  68.5 us (38%)
  Pallas kernels  53.9 us (30%)
  waiting for transfers between devices  46.6 us (26%)
  local copies, waits for them, and re-layouts  8.31 us (5%)
  other arithmetic  3.01 us (2%)
    ppermute x35, starting transfers between devices, rotate(): lax.ppermute(value, axis, [(i, (i + shift) % size) for i in range(size)])  46.9 us
    ppermute x35, waiting for transfers between devices, rotate(): lax.ppermute(value, axis, [(i, (i + shift) % size) for i in range(size)])  36.9 us
    pallas_call x4, Pallas kernels, sums(): pl.pallas_call(kernel, out_shape=[jax.ShapeDtypeStruct(shape, F32 if shap...  11.1 us
    pallas_call x1, Pallas kernels, attend(): pl.pallas_call(attend_kernel, out_shape=shapes, in_specs=[SMEM] + [VMEM]...  10.2 us
    all_to_all x1, waiting for transfers between devices, per_device(): merges = lax.all_to_all(merges, LAT + ('xl',), 0, 0)  9.65 us
    pallas_call x1, Pallas kernels, hidden_units(): pl.pallas_call(hidden_kernel, out_shape=out, in_specs=[VMEM] * 16, out_sp...  8.59 us
    all_to_all x1, starting transfers between devices, per_device(): blocks = lax.all_to_all(blocks, LAT + ('xl',), 0, 0)  6.91 us
    all_to_all x1, starting transfers between devices, per_device(): merges = lax.all_to_all(merges, LAT + ('xl',), 0, 0)  6.88 us
  transfers between devices with their start and end apart: 39, of which 16 were waited for; matrix products, arithmetic and copies ran while one was open for 3% of the time, Pallas kernels for 24%

profile of v2, /device:TPU:1, one launch (start us, length us, event | category | flops | bytes accessed | tf_op | source)
XLA Modules:
  0.0 181.3 jit_solution(15324841557497746472)
XLA Ops:
  0.6 1.0 fusion.13
  1.6 2.5 %collective-permute-start = (bf16[4,32,512]{2,1,0:T(8,128)(2,1)S(1)}, bf16[4,32,512]{2,1,0:T(8,128)(2,1)S(1)}, u32[]{:S(2)}, u32[]{:S(2)}) collective-permute-start(bf16[4,32,512]{2,1,0:T(8,128)(2,1)S(1)} %get-tuple-element.188), channel_id=1, source_target_pairs={{0,16},{16,32},{32,48},{48,64},{64,80},{80,96},{96,112},{112,0},{1... | collective-permute-start | bytes 393224 | tf_op jit(solution)/shard_map/ppermute | solution.py:23
  4.2 4.7 %collective-permute-start.1 = (bf16[4,32,512]{2,1,0:T(8,128)(2,1)S(1)}, bf16[4,32,512]{2,1,0:T(8,128)(2,1)S(1)}, u32[]{:S(2)}, u32[]{:S(2)}) collective-permute-start(bf16[4,32,512]{2,1,0:T(8,128)(2,1)S(1)} %get-tuple-element.187), channel_id=1, source_target_pairs={{0,112},{16,0},{32,16},{48,32},{64,48},{80,64},{96,80},{112,96},{1... | collective-permute-start | bytes 393224 | tf_op jit(solution)/shard_map/ppermute | solution.py:23
  8.8 1.0 fusion.12
  9.8 2.1 %collective-permute-done.top_ref = bf16[4,32,512]{2,1,0:T(8,128)(2,1)S(1)} collective-permute-done((bf16[4,32,512]{2,1,0:T(8,128)(2,1)S(1)}, bf16[4,32,512]{2,1,0:T(8,128)(2,1)S(1)}, u32[]{:S(2)}, u32[]{:S(2)}) %collective-permute-start) | collective-permute-done | bytes 131104 | tf_op jit(solution)/shard_map/ppermute | solution.py:23
  12.1 1.3 collective-permute-start.3
  14.0 2.1 %collective-permute-done.3.right_ref = bf16[24,4,512]{2,1,0:T(4,128)(2,1)S(1)} collective-permute-done((bf16[24,4,512]{2,1,0:T(4,128)(2,1)S(1)}, bf16[24,4,512]{2,1,0:T(4,128)(2,1)S(1)}, u32[]{:S(2)}, u32[]{:S(2)}) %collective-permute-start.3) | collective-permute-done | bytes 98336 | tf_op jit(solution)/shard_map/ppermute | solution.py:23
  16.2 2.6 %collective-permute-start.4 = (bf16[1024,256]{1,0:T(8,128)(2,1)}, bf16[1024,256]{1,0:T(8,128)(2,1)}, u32[]{:S(2)}, u32[]{:S(2)}) collective-permute-start(bf16[1024,256]{1,0:T(8,128)(2,1)} %refs_8_.1), channel_id=1, source_target_pairs={{0,2},{2,0},{1,3},{3,1},{4,6},{6,4},{5,7},{7,5},{8,10},{10,8},{9,1... | collective-permute-start | bytes 1572872 | tf_op jit(solution)/shard_map/ppermute | solution.py:23
  18.8 2.8 %collective-permute-start.5 = (bf16[1024,256]{1,0:T(8,128)(2,1)}, bf16[1024,256]{1,0:T(8,128)(2,1)S(1)}, u32[]{:S(2)}, u32[]{:S(2)}) collective-permute-start(bf16[1024,256]{1,0:T(8,128)(2,1)} %refs_8_.1), channel_id=1, source_target_pairs={{0,1},{1,0},{2,3},{3,2},{4,5},{5,4},{6,7},{7,6},{8,9},{9,8},{10,11... | collective-permute-start | bytes 1572872 | tf_op jit(solution)/shard_map/ppermute | solution.py:23
  21.6 1.4 collective-permute-start.7
  23.0 1.3 collective-permute-start.8
  24.3 0.6 stack.42.place_ref.refs_0_.place
  24.9 10.2 %shard_map.145 = (bf16[128,1024]{1,0:T(8,128)(2,1)}, bf16[128,1024]{1,0:T(8,128)(2,1)}, bf16[128,2048]{1,0:T(8,128)(2,1)}, bf16[4,128,512]{2,1,0:T(8,128)(2,1)}, bf16[128,2048]{1,0:T(8,128)(2,1)}) custom-call(s32[7]{0:T(128)} %stack.42.place_ref.refs_0_.place, bf16[16,32,512]{2,1,0:T(8,128)(2,1)} %own_ref.1, bf16[4,32,512]{2,1,0:T(8,128)(2,1)} %copy-done.25, ...), custom_call_target="tpu_custom_call" | custom-call | flops 1000 | bytes 1000 | tf_op jit(solution)/shard_map/pallas_call | solution.py:168
  35.2 1.3 collective-permute-done.6.refs_5_.refs_6_
  37.5 1.2 collective-permute-start.12
  38.7 1.7 collective-permute-start.13
  40.4 0.6 collective-permute-start.10
  41.1 1.7 collective-permute-start.11
  43.1 6.4 %collective-permute-done.10.refs_2_.refs_3_ = bf16[128,1024]{1,0:T(8,128)(2,1)S(1)} collective-permute-done((bf16[128,1024]{1,0:T(8,128)(2,1)}, bf16[128,1024]{1,0:T(8,128)(2,1)S(1)}, u32[]{:S(2)}, u32[]{:S(2)}) %collective-permute-start.10) | collective-permute-done | bytes 262176 | tf_op jit(solution)/shard_map/ppermute | solution.py:23
  49.6 5.4 %collective-permute-done.11.refs_3_.refs_4_ = bf16[128,1024]{1,0:T(8,128)(2,1)S(1)} collective-permute-done((bf16[128,1024]{1,0:T(8,128)(2,1)}, bf16[128,1024]{1,0:T(8,128)(2,1)S(1)}, u32[]{:S(2)}, u32[]{:S(2)}) %collective-permute-start.11) | collective-permute-done | bytes 262176 | tf_op jit(solution)/shard_map/ppermute | solution.py:23
  54.9 1.0 collective-permute-done.9.refs_1_.refs_2_
  57.4 3.7 %all-to-all-start = ((bf16[4,128,512]{2,1,0:T(8,128)(2,1)}), bf16[4,128,512]{2,1,0:T(8,128)(2,1)S(1)}, u32[]{:S(2)}, u32[]{:S(2)}) async-start(bf16[4,128,512]{2,1,0:T(8,128)(2,1)} %get-tuple-element.124), calls=%async_computation | async-start | bytes 1048576 | tf_op jit(solution)/shard_map/all_to_all | solution.py:527
  61.0 0.8 copy-done.8
  61.9 8.6 %shard_map.146 = (bf16[128,1024]{1,0:T(8,128)(2,1)}, bf16[128,1024]{1,0:T(8,128)(2,1)}, bf16[128,1024]{1,0:T(8,128)(2,1)}, bf16[128,1024]{1,0:T(8,128)(2,1)}, bf...) custom-call(bf16[128,1024]{1,0:T(8,128)(2,1)} %get-tuple-element.106.refs_0_.refs_1_, bf16[128,1024]{1,0:T(8,128)(2,1)} %copy-done.14, ...), custom_call_target="tpu_custom_call" | custom-call | flops 1000 | bytes 1000 | tf_op jit(solution)/shard_map/pallas_call | solution.py:226
  70.5 6.2 %shard_map.147 = (bf16[16,256,256]{2,1,0:T(8,128)(2,1)}, bf16[16,256,256]{2,1,0:T(8,128)(2,1)}) custom-call(s32[7]{0:T(128)} %stack.42.place_ref.refs_0_.place, bf16[128,1024]{1,0:T(8,128)(2,1)} %get-tuple-element.106.refs_0_.refs_1_, bf16[128,1024]{1,0:T(8,128)(2,1)} %copy-done.14, bf16[128,1024]{1,0:T(8,128)(2,1)} %copy-done.12, ...), custom_call_target="tpu_custom_call" | custom-call | flops 1000 | bytes 1000 | tf_op jit(solution)/shard_map/pallas_call | solution.py:264
  76.7 0.7 collective-permute-start.16
  77.5 2.3 %collective-permute-start.17 = (bf16[128,1024]{1,0:T(8,128)(2,1)}, bf16[128,1024]{1,0:T(8,128)(2,1)S(1)}, u32[]{:S(2)}, u32[]{:S(2)}) collective-permute-start(bf16[128,1024]{1,0:T(8,128)(2,1)} %get-tuple-element.132), channel_id=1, source_target_pairs={{0,12},{4,0},{8,4},{12,8},{1,13},{5,1},{9,5},{13,9},{2,14},{6,2},{... | collective-permute-start | bytes 786440 | tf_op jit(solution)/shard_map/ppermute | solution.py:23
  81.5 4.0 %shard_map.148 = bf16[16,256,256]{2,1,0:T(8,128)(2,1)} custom-call(bf16[16,256,256]{2,1,0:T(8,128)(2,1)} %get-tuple-element.127.keep, bf16[16,256,256]{2,1,0:T(8,128)(2,1)} %collective-permute-done.16.got), custom_call_target="tpu_custom_call" | custom-call | flops 1000 | bytes 1000 | tf_op jit(solution)/shard_map/pallas_call | solution.py:311
  85.6 6.9 %all-to-all-start.1 = ((bf16[16,256,256]{2,1,0:T(8,128)(2,1)}), bf16[16,256,256]{2,1,0:T(8,128)(2,1)}, u32[]{:S(2)}, u32[]{:S(2)}) async-start(bf16[16,256,256]{2,1,0:T(8,128)(2,1)} %shard_map.148), calls=%async_computation.1 | async-start | bytes 4194304 | tf_op jit(solution)/shard_map/all_to_all | solution.py:542
  92.5 3.9 %shard_map.149 = (bf16[128,1024]{1,0:T(8,128)(2,1)}, bf16[128,1024]{1,0:T(8,128)(2,1)}, bf16[128,1024]{1,0:T(8,128)(2,1)}, bf16[128,1024]{1,0:T(8,128)(2,1)}) custom-call(bf16[512,1024]{1,0:T(8,128)(2,1)} %get-tuple-element.125.refs_9_.refs_0_, bf16[256,1024]{1,0:T(8,128)(2,1)} %refs_1_.1, bf16[256,1024]{1,0:T(8,128)(2,1)} %copy-done.8, ...), custom_call_target="tpu_custom_call" | custom-call | flops 1000 | bytes 1000 | tf_op jit(solution)/shard_map/pallas_call | solution.py:341
  97.0 1.3 collective-permute-start.20
  98.3 2.2 %collective-permute-start.21 = (bf16[128,1024]{1,0:T(8,128)(2,1)S(1)}, bf16[128,1024]{1,0:T(8,128)(2,1)S(1)}, u32[]{:S(2)}, u32[]{:S(2)}) collective-permute-start(bf16[128,1024]{1,0:T(8,128)(2,1)S(1)} %fusion.8.coarse_grad.right0), channel_id=1, source_target_pairs={{0,8},{4,12},{8,0},{12,4},{1,9},{5,13},{9,1},{13,5},{2,10},{6,14},... | collective-permute-start | bytes 786440 | tf_op jit(solution)/shard_map/ppermute | solution.py:23
  100.6 1.2 collective-permute-start.22
  101.7 6.0 %shard_map.150 = (bf16[16,32,512]{2,1,0:T(8,128)(2,1)}, bf16[2,8,16,256]{3,2,1,0:T(8,128)(2,1)}, bf16[2,8,16,256]{3,2,1,0:T(8,128)(2,1)}, bf16[2,8,16,256]{3,2,1,0:T(8,128)(2,1)}, bf16[2,8,16,256]{3,2,1,0:T(8,128)(2,1)}) custom-call(s32[7]{0:T(128)} %stack.42.place_ref.refs_0_.place, bf16[128,1024]{1,0:T(8,128)(2,1)} %copy-done.4, f32[1,2048]{1,0:T(1,128)} %bitcast.31, ...), custom_call_target="tpu_custom_call" | custom-call | flops 1000 | bytes 1000 | tf_op jit(solution)/shard_map/pallas_call | solution.py:473
  108.1 0.9 collective-permute-start.25
  109.0 1.6 collective-permute-start.26
  110.5 1.5 collective-permute-done.21.right2
  112.0 0.7 copy-done.22
  112.8 3.2 %shard_map.151 = (bf16[16,16,1024]{2,1,0:T(8,128)(2,1)}, bf16[16,16,1024]{2,1,0:T(8,128)(2,1)}) custom-call(s32[7]{0:T(128)} %stack.42.place_ref.refs_0_.place, bf16[4,128,512]{2,1,0:T(8,128)(2,1)} %copy-done.6, bf16[128,1024]{1,0:T(8,128)(2,1)} %copy-done.4, bf16[128,1024]{1,0:T(8,128)(2,1)} %copy-done.21, bf16[128,1024]{1,0:T(8,128)(2,1)} %copy-done.22, ...), custom_call_target="tpu_custom_call" | custom-call | flops 1000 | bytes 1000 | tf_op jit(solution)/shard_map/pallas_call | solution.py:366
  116.0 2.6 %collective-permute-start.23 = (bf16[16,16,1024]{2,1,0:T(8,128)(2,1)}, bf16[16,16,1024]{2,1,0:T(8,128)(2,1)S(1)}, u32[]{:S(2)}, u32[]{:S(2)}) collective-permute-start(bf16[16,16,1024]{2,1,0:T(8,128)(2,1)} %get-tuple-element.150), channel_id=1, source_target_pairs={{0,1},{1,0},{2,3},{3,2},{4,5},{5,4},{6,7},{7,6},{8,9},{9,8},{10,11... | collective-permute-start | bytes 1572872 | tf_op jit(solution)/shard_map/ppermute | solution.py:23
  118.6 1.0 add_convert_fusion
  119.6 0.6 slice_bitcast_fusion
  120.7 0.9 collective-permute-done.27.proj_got
  121.6 0.6 copy-done.29
  122.4 2.2 %shard_map.152 = bf16[16,80,256]{2,1,0:T(8,128)(2,1)} custom-call(bf16[16,16,1024]{2,1,0:T(8,128)(2,1)} %get-tuple-element.149.merge_keep, bf16[16,16,1024]{2,1,0:T(8,128)(2,1)} %copy-done.18, bf16[8,16,256]{2,1,0:T(8,128)(2,1)} %get-tuple-element.190.proj_keep, bf16[8,16,256]{2,1,0:T(8,128)(2,1)} %copy-done.29), custom_call_target="tpu_custom_call" | custom-call | flops 1000 | bytes 1000 | tf_op jit(solution)/shard_map/pallas_call | solution.py:311
  124.6 6.9 %all-to-all-start.2 = ((bf16[16,80,256]{2,1,0:T(8,128)(2,1)}), bf16[16,80,256]{2,1,0:T(8,128)(2,1)S(1)}, u32[]{:S(2)}, u32[]{:S(2)}) async-start(bf16[16,80,256]{2,1,0:T(8,128)(2,1)} %shard_map.152), calls=%async_computation.2 | async-start | bytes 1310720 | tf_op jit(solution)/shard_map/all_to_all | solution.py:560
  131.5 2.6 %shard_map.153.total = bf16[256,256]{1,0:T(8,128)(2,1)} custom-call(bf16[16,256,256]{2,1,0:T(8,128)(2,1)} %all-to-all-done.1.blocks), custom_call_target="tpu_custom_call" | custom-call | flops 1000 | bytes 1000 | tf_op jit(solution)/shard_map/pallas_call | solution.py:311
  134.1 9.6 %all-to-all-done.2.merges = bf16[16,80,256]{2,1,0:T(8,128)(2,1)S(1)} async-done(((bf16[16,80,256]{2,1,0:T(8,128)(2,1)}), bf16[16,80,256]{2,1,0:T(8,128)(2,1)S(1)}, u32[]{:S(2)}, u32[]{:S(2)}) %all-to-all-start.2) | async-done | bytes 655392 | tf_op jit(solution)/shard_map/all_to_all | solution.py:560
  143.7 0.8 copy-done.2
  144.5 2.3 %shard_map.154 = (bf16[8,272,256]{2,1,0:T(8,128)(2,1)}, f32[16,1024]{1,0:T(8,128)}) custom-call(bf16[256,256]{1,0:T(8,128)(2,1)} %shard_map.153.total, bf16[16,80,256]{2,1,0:T(8,128)(2,1)} %copy-done.2), custom_call_target="tpu_custom_call" | custom-call | flops 1000 | bytes 1000 | tf_op jit(solution)/shard_map/pallas_call | solution.py:311
  146.9 4.1 %all-to-all-start.3 = ((bf16[8,272,256]{2,1,0:T(8,128)(2,1)}), bf16[8,272,256]{2,1,0:T(8,128)(2,1)S(1)}, u32[]{:S(2)}, u32[]{:S(2)}) async-start(bf16[8,272,256]{2,1,0:T(8,128)(2,1)} %get-tuple-element.167), calls=%async_computation.3 | async-start | bytes 2228224 | tf_op jit(solution)/shard_map/all_to_all | solution.py:565
  151.0 1.9 %collective-permute-start.28 = (bf16[128,1024]{1,0:T(8,128)(2,1)}, bf16[128,1024]{1,0:T(8,128)(2,1)S(1)}, u32[]{:S(2)}, u32[]{:S(2)}) collective-permute-start(bf16[128,1024]{1,0:T(8,128)(2,1)} %get-tuple-element.169), channel_id=1, source_target_pairs={{0,12},{4,0},{8,4},{12,8},{1,13},{5,1},{9,5},{13,9},{2,14},{6,2},{... | collective-permute-start | bytes 786440 | tf_op jit(solution)/shard_map/ppermute | solution.py:23
  152.9 1.6 collective-permute-start.29
  154.4 3.8 %collective-permute-done.28 = bf16[128,1024]{1,0:T(8,128)(2,1)S(1)} collective-permute-done((bf16[128,1024]{1,0:T(8,128)(2,1)}, bf16[128,1024]{1,0:T(8,128)(2,1)S(1)}, u32[]{:S(2)}, u32[]{:S(2)}) %collective-permute-start.28) | collective-permute-done | bytes 262176 | tf_op jit(solution)/shard_map/ppermute | solution.py:23
  158.3 2.7 %collective-permute-done.29 = bf16[128,1024]{1,0:T(8,128)(2,1)S(1)} collective-permute-done((bf16[128,1024]{1,0:T(8,128)(2,1)}, bf16[128,1024]{1,0:T(8,128)(2,1)S(1)}, u32[]{:S(2)}, u32[]{:S(2)}) %collective-permute-start.29) | collective-permute-done | bytes 262176 | tf_op jit(solution)/shard_map/ppermute | solution.py:23
  161.0 7.5 %collective-permute-done.30 = bf16[128,1024]{1,0:T(8,128)(2,1)S(1)} collective-permute-done((bf16[128,1024]{1,0:T(8,128)(2,1)S(1)}, bf16[128,1024]{1,0:T(8,128)(2,1)S(1)}, u32[]{:S(2)}, u32[]{:S(2)}) %collective-permute-start.30) | collective-permute-done | bytes 262176 | tf_op jit(solution)/shard_map/ppermute | solution.py:23
  168.4 0.9 fusion.10
  169.5 1.0 collective-permute-start.32
  170.4 2.0 %collective-permute-start.33 = (bf16[8,16,256]{2,1,0:T(8,128)(2,1)S(1)}, bf16[8,16,256]{2,1,0:T(8,128)(2,1)S(1)}, u32[]{:S(2)}, u32[]{:S(2)}) collective-permute-start(bf16[8,16,256]{2,1,0:T(8,128)(2,1)S(1)} %get-tuple-element.184), channel_id=1, source_target_pairs={{0,12},{4,0},{8,4},{12,8},{1,13},{5,1},{9,5},{13,9},{2,14},{6,2},{... | collective-permute-start | bytes 196616 | tf_op jit(solution)/shard_map/ppermute | solution.py:23
  172.4 2.7 %shard_map.155 = (f32[1024,256]{1,0:T(8,128)}, f32[256,1024]{1,0:T(8,128)}) custom-call(bf16[8,272,256]{2,1,0:T(8,128)(2,1)} %copy-done.1), custom_call_target="tpu_custom_call" | custom-call | flops 1000 | bytes 1000 | tf_op jit(solution)/shard_map/pallas_call | solution.py:390
  175.5 1.7 collective-permute-start.34
  177.3 1.2 collective-permute-done.34.other
  178.5 0.7 copy-done.24
  179.2 2.1 %shard_map.156 = f32[512,512]{1,0:T(8,128)} custom-call(s32[7]{0:T(128)} %stack.42.place_ref.refs_0_.place, bf16[4,8,16,256]{3,2,1,0:T(8,128)(2,1)} %copy-done.15, bf16[4,8,16,256]{3,2,1,0:T(8,128)(2,1)} %copy-done.24), custom_call_target="tpu_custom_call" | custom-call | flops 1000 | bytes 1000 | tf_op jit(solution)/shard_map/pallas_call | solution.py:416
  (111 shorter events, 7.5 us)
Async XLA Ops:
  1.6 10.3 %collective-permute-start = (bf16[4,32,512]{2,1,0:T(8,128)(2,1)S(1)}, bf16[4,32,512]{2,1,0:T(8,128)(2,1)S(1)}, u32[]{:S(2)}, u32[]{:S(2)}) collective-permute-start(bf16[4,32,512]{2,1,0:T(8,128)(2,1)S(1)} %get-tuple-element.188), channel_id=1, source_target_pairs={{0,16},{16,32},{32,48},{48,64},{64,80},{80,96},{96,112},{112,0},{1... | collective-permute-start | bytes 393224 | tf_op jit(solution)/shard_map/ppermute | solution.py:23
  4.2 7.8 %collective-permute-start.1 = (bf16[4,32,512]{2,1,0:T(8,128)(2,1)S(1)}, bf16[4,32,512]{2,1,0:T(8,128)(2,1)S(1)}, u32[]{:S(2)}, u32[]{:S(2)}) collective-permute-start(bf16[4,32,512]{2,1,0:T(8,128)(2,1)S(1)} %get-tuple-element.187), channel_id=1, source_target_pairs={{0,112},{16,0},{32,16},{48,32},{64,48},{80,64},{96,80},{112,96},{1... | collective-permute-start | bytes 393224 | tf_op jit(solution)/shard_map/ppermute | solution.py:23
  12.0 13.0 %copy-start.25 = (bf16[4,32,512]{2,1,0:T(8,128)(2,1)}, bf16[4,32,512]{2,1,0:T(8,128)(2,1)S(1)}, u32[]{:S(2)}) copy-start(bf16[4,32,512]{2,1,0:T(8,128)(2,1)S(1)} %collective-permute-done.top_ref) | copy-start | bytes 393220
  12.0 9.6 %copy-start.26 = (bf16[4,32,512]{2,1,0:T(8,128)(2,1)}, bf16[4,32,512]{2,1,0:T(8,128)(2,1)S(1)}, u32[]{:S(2)}) copy-start(bf16[4,32,512]{2,1,0:T(8,128)(2,1)S(1)} %collective-permute-done.1.bottom_ref) | copy-start | bytes 393220
  12.1 4.1 %collective-permute-start.3 = (bf16[24,4,512]{2,1,0:T(4,128)(2,1)S(1)}, bf16[24,4,512]{2,1,0:T(4,128)(2,1)S(1)}, u32[]{:S(2)}, u32[]{:S(2)}) collective-permute-start(bf16[24,4,512]{2,1,0:T(4,128)(2,1)S(1)} %pad_maximum_fusion.2), channel_id=1, source_target_pairs={{0,15},{1,0},{2,1},{3,2},{4,3},{5,4},{6,5},{7,6},{8,7},{9,8},{10,9... | collective-permute-start | bytes 294920 | tf_op jit(solution)/shard_map/ppermute | solution.py:23
  13.5 2.8 %collective-permute-start.2 = (bf16[24,4,512]{2,1,0:T(4,128)(2,1)S(1)}, bf16[24,4,512]{2,1,0:T(4,128)(2,1)S(1)}, u32[]{:S(2)}, u32[]{:S(2)}) collective-permute-start(bf16[24,4,512]{2,1,0:T(4,128)(2,1)S(1)} %pad_maximum_fusion.1), channel_id=1, source_target_pairs={{0,1},{1,2},{2,3},{3,4},{4,5},{5,6},{6,7},{7,8},{8,9},{9,10},{10,1... | collective-permute-start | bytes 294920 | tf_op jit(solution)/shard_map/ppermute | solution.py:23
  16.2 6.8 %copy-start.27 = (bf16[24,4,512]{2,1,0:T(4,128)(2,1)}, bf16[24,4,512]{2,1,0:T(4,128)(2,1)S(1)}, u32[]{:S(2)}) copy-start(bf16[24,4,512]{2,1,0:T(4,128)(2,1)S(1)} %collective-permute-done.3.right_ref) | copy-start | bytes 294916
  16.2 8.1 %copy-start.28 = (bf16[24,4,512]{2,1,0:T(4,128)(2,1)}, bf16[24,4,512]{2,1,0:T(4,128)(2,1)S(1)}, u32[]{:S(2)}) copy-start(bf16[24,4,512]{2,1,0:T(4,128)(2,1)S(1)} %collective-permute-done.2.left_ref) | copy-start | bytes 294916
  16.2 20.6 %collective-permute-start.4 = (bf16[1024,256]{1,0:T(8,128)(2,1)}, bf16[1024,256]{1,0:T(8,128)(2,1)}, u32[]{:S(2)}, u32[]{:S(2)}) collective-permute-start(bf16[1024,256]{1,0:T(8,128)(2,1)} %refs_8_.1), channel_id=1, source_target_pairs={{0,2},{2,0},{1,3},{3,1},{4,6},{6,4},{5,7},{7,5},{8,10},{10,8},{9,1... | collective-permute-start | bytes 1572872 | tf_op jit(solution)/shard_map/ppermute | solution.py:23
  18.8 18.0 %collective-permute-start.5 = (bf16[1024,256]{1,0:T(8,128)(2,1)}, bf16[1024,256]{1,0:T(8,128)(2,1)S(1)}, u32[]{:S(2)}, u32[]{:S(2)}) collective-permute-start(bf16[1024,256]{1,0:T(8,128)(2,1)} %refs_8_.1), channel_id=1, source_target_pairs={{0,1},{1,0},{2,3},{3,2},{4,5},{5,4},{6,7},{7,6},{8,9},{9,8},{10,11... | collective-permute-start | bytes 1572872 | tf_op jit(solution)/shard_map/ppermute | solution.py:23
  21.6 14.9 %collective-permute-start.6 = (bf16[128,1024]{1,0:T(8,128)(2,1)}, bf16[128,1024]{1,0:T(8,128)(2,1)S(1)}, u32[]{:S(2)}, u32[]{:S(2)}) collective-permute-start(bf16[128,1024]{1,0:T(8,128)(2,1)} %bitcast.20), channel_id=1, source_target_pairs={{0,4},{4,8},{8,12},{12,0},{1,5},{5,9},{9,13},{13,1},{2,6},{6,10},{... | collective-permute-start | bytes 786440 | tf_op jit(solution)/shard_map/ppermute | solution.py:23
  21.6 14.9 %collective-permute-start.7 = (bf16[128,1024]{1,0:T(8,128)(2,1)}, bf16[128,1024]{1,0:T(8,128)(2,1)S(1)}, u32[]{:S(2)}, u32[]{:S(2)}) collective-permute-start(bf16[128,1024]{1,0:T(8,128)(2,1)} %bitcast.21), channel_id=1, source_target_pairs={{0,8},{4,12},{8,0},{12,4},{1,9},{5,13},{9,1},{13,5},{2,10},{6,14},... | collective-permute-start | bytes 786440 | tf_op jit(solution)/shard_map/ppermute | solution.py:23
  23.0 13.8 %collective-permute-start.8 = (bf16[128,1024]{1,0:T(8,128)(2,1)}, bf16[128,1024]{1,0:T(8,128)(2,1)S(1)}, u32[]{:S(2)}, u32[]{:S(2)}) collective-permute-start(bf16[128,1024]{1,0:T(8,128)(2,1)} %bitcast.22), channel_id=1, source_target_pairs={{0,12},{4,0},{8,4},{12,8},{1,13},{5,1},{9,5},{13,9},{2,14},{6,2},{... | collective-permute-start | bytes 786440 | tf_op jit(solution)/shard_map/ppermute | solution.py:23
  24.9 13.7 %copy-start.5 = (bf16[256,1024]{1,0:T(8,128)(2,1)S(1)}, bf16[256,1024]{1,0:T(8,128)(2,1)}, u32[]{:S(2)}) copy-start(bf16[256,1024]{1,0:T(8,128)(2,1)} %refs_1_.1) | copy-start | bytes 1572868
  36.5 25.4 %copy-start.9 = (bf16[128,1024]{1,0:T(8,128)(2,1)}, bf16[128,1024]{1,0:T(8,128)(2,1)S(1)}, u32[]{:S(2)}) copy-start(bf16[128,1024]{1,0:T(8,128)(2,1)S(1)} %collective-permute-done.6.refs_5_.refs_6_) | copy-start | bytes 786436
  36.8 1.9 %copy-start.16 = (bf16[1024,256]{1,0:T(8,128)(2,1)}, bf16[1024,256]{1,0:T(8,128)(2,1)S(1)}, u32[]{:S(2)}) copy-start(bf16[1024,256]{1,0:T(8,128)(2,1)S(1)} %collective-permute-done.5.refs_9_) | copy-start | bytes 1572868
  37.5 18.5 %collective-permute-start.12 = (bf16[1024,256]{1,0:T(8,128)(2,1)}, bf16[1024,256]{1,0:T(8,128)(2,1)S(1)}, u32[]{:S(2)}, u32[]{:S(2)}) collective-permute-start(bf16[1024,256]{1,0:T(8,128)(2,1)} %collective-permute-done.4.refs_10_), channel_id=1, source_target_pairs={{0,1},{1,0},{2,3},{3,2},{4,5},{5,4},{6,7},{7,6},{8,9},{9,8},{10,11... | collective-permute-start | bytes 1572872 | tf_op jit(solution)/shard_map/ppermute | solution.py:23
  38.7 17.3 %collective-permute-start.13 = (bf16[256,1024]{1,0:T(8,128)(2,1)S(1)}, bf16[256,1024]{1,0:T(8,128)(2,1)S(1)}, u32[]{:S(2)}, u32[]{:S(2)}) collective-permute-start(bf16[256,1024]{1,0:T(8,128)(2,1)S(1)} %copy-done.5), channel_id=1, source_target_pairs={{0,2},{2,0},{1,3},{3,1},{4,6},{6,4},{5,7},{7,5},{8,10},{10,8},{9,1... | collective-permute-start | bytes 1572872 | tf_op jit(solution)/shard_map/ppermute | solution.py:23
  40.4 9.2 %collective-permute-start.10 = (bf16[128,1024]{1,0:T(8,128)(2,1)}, bf16[128,1024]{1,0:T(8,128)(2,1)S(1)}, u32[]{:S(2)}, u32[]{:S(2)}) collective-permute-start(bf16[128,1024]{1,0:T(8,128)(2,1)} %get-tuple-element.106.refs_0_.refs_1_), channel_id=1, source_target_pairs={{0,8},{4,12},{8,0},{12,4},{1,9},{5,13},{9,1},{13,5},{2,10},{6,14},... | collective-permute-start | bytes 786440 | tf_op jit(solution)/shard_map/ppermute | solution.py:23
  41.1 13.9 %collective-permute-start.11 = (bf16[128,1024]{1,0:T(8,128)(2,1)}, bf16[128,1024]{1,0:T(8,128)(2,1)S(1)}, u32[]{:S(2)}, u32[]{:S(2)}) collective-permute-start(bf16[128,1024]{1,0:T(8,128)(2,1)} %get-tuple-element.106.refs_0_.refs_1_), channel_id=1, source_target_pairs={{0,12},{4,0},{8,4},{12,8},{1,13},{5,1},{9,5},{13,9},{2,14},{6,2},{... | collective-permute-start | bytes 786440 | tf_op jit(solution)/shard_map/ppermute | solution.py:23
  42.8 13.2 %collective-permute-start.9 = (bf16[128,1024]{1,0:T(8,128)(2,1)}, bf16[128,1024]{1,0:T(8,128)(2,1)S(1)}, u32[]{:S(2)}, u32[]{:S(2)}) collective-permute-start(bf16[128,1024]{1,0:T(8,128)(2,1)} %get-tuple-element.106.refs_0_.refs_1_), channel_id=1, source_target_pairs={{0,4},{4,8},{8,12},{12,0},{1,5},{5,9},{9,13},{13,1},{2,6},{6,10},{... | collective-permute-start | bytes 786440 | tf_op jit(solution)/shard_map/ppermute | solution.py:23
  49.6 7.8 %copy-start.12 = (bf16[128,1024]{1,0:T(8,128)(2,1)}, bf16[128,1024]{1,0:T(8,128)(2,1)S(1)}, u32[]{:S(2)}) copy-start(bf16[128,1024]{1,0:T(8,128)(2,1)S(1)} %collective-permute-done.10.refs_2_.refs_3_) | copy-start | bytes 786436
  54.9 2.4 %copy-start.13 = (bf16[128,1024]{1,0:T(8,128)(2,1)}, bf16[128,1024]{1,0:T(8,128)(2,1)S(1)}, u32[]{:S(2)}) copy-start(bf16[128,1024]{1,0:T(8,128)(2,1)S(1)} %collective-permute-done.11.refs_3_.refs_4_) | copy-start | bytes 786436
  56.0 0.9 copy-start.17
  56.0 5.9 %copy-start.7 = (bf16[256,1024]{1,0:T(8,128)(2,1)}, bf16[256,1024]{1,0:T(8,128)(2,1)S(1)}, u32[]{:S(2)}) copy-start(bf16[256,1024]{1,0:T(8,128)(2,1)S(1)} %collective-permute-done.13.refs_14_.refs_3_) | copy-start | bytes 1572868
  56.0 5.0 %collective-permute-start.14 = (bf16[256,1024]{1,0:T(8,128)(2,1)S(1)}, bf16[256,1024]{1,0:T(8,128)(2,1)S(1)}, u32[]{:S(2)}, u32[]{:S(2)}) collective-permute-start(bf16[256,1024]{1,0:T(8,128)(2,1)S(1)} %copy-done.5), channel_id=1, source_target_pairs={{0,1},{1,0},{2,3},{3,2},{4,5},{5,4},{6,7},{7,6},{8,9},{9,8},{10,11... | collective-permute-start | bytes 1572872 | tf_op jit(solution)/shard_map/ppermute | solution.py:23
  56.9 5.0 %collective-permute-start.15 = (bf16[256,1024]{1,0:T(8,128)(2,1)S(1)}, bf16[256,1024]{1,0:T(8,128)(2,1)}, u32[]{:S(2)}, u32[]{:S(2)}) collective-permute-start(bf16[256,1024]{1,0:T(8,128)(2,1)S(1)} %collective-permute-done.13.refs_14_.refs_3_), channel_id=1, source_target_pairs={{0,1},{1,0},{2,3},{3,2},{4,5},{5,4},{6,7},{7,6},{8,9},{9,8},{10,11... | collective-permute-start | bytes 1572872 | tf_op jit(solution)/shard_map/ppermute | solution.py:23
  57.4 13.1 %all-to-all-start = ((bf16[4,128,512]{2,1,0:T(8,128)(2,1)}), bf16[4,128,512]{2,1,0:T(8,128)(2,1)S(1)}, u32[]{:S(2)}, u32[]{:S(2)}) async-start(bf16[4,128,512]{2,1,0:T(8,128)(2,1)} %get-tuple-element.124), calls=%async_computation | async-start | bytes 1048576 | tf_op jit(solution)/shard_map/all_to_all | solution.py:527
  61.0 0.8 copy-start.8
  70.5 6.2 %copy-start.6 = (bf16[4,128,512]{2,1,0:T(8,128)(2,1)}, bf16[4,128,512]{2,1,0:T(8,128)(2,1)S(1)}, u32[]{:S(2)}) copy-start(bf16[4,128,512]{2,1,0:T(8,128)(2,1)S(1)} %all-to-all-done.left) | copy-start | bytes 1572868
  70.5 6.9 %copy-start = (bf16[128,1024]{1,0:T(8,128)(2,1)S(1)}, bf16[128,1024]{1,0:T(8,128)(2,1)}, u32[]{:S(2)}) copy-start(bf16[128,1024]{1,0:T(8,128)(2,1)} %get-tuple-element.130) | copy-start | bytes 786436
  70.5 10.0 %copy-start.32 = (bf16[128,1024]{1,0:T(8,128)(2,1)S(1)}, bf16[128,1024]{1,0:T(8,128)(2,1)}, u32[]{:S(2)}) copy-start(bf16[128,1024]{1,0:T(8,128)(2,1)} %get-tuple-element.134) | copy-start | bytes 786436
  76.7 4.9 %collective-permute-start.16 = (bf16[16,256,256]{2,1,0:T(8,128)(2,1)}, bf16[16,256,256]{2,1,0:T(8,128)(2,1)}, u32[]{:S(2)}, u32[]{:S(2)}) collective-permute-start(bf16[16,256,256]{2,1,0:T(8,128)(2,1)} %get-tuple-element.128), channel_id=1, source_target_pairs={{0,1},{1,0},{2,3},{3,2},{4,5},{5,4},{6,7},{7,6},{8,9},{9,8},{10,11... | collective-permute-start | bytes 6291464 | tf_op jit(solution)/shard_map/ppermute | solution.py:23
  77.5 18.8 %collective-permute-start.17 = (bf16[128,1024]{1,0:T(8,128)(2,1)}, bf16[128,1024]{1,0:T(8,128)(2,1)S(1)}, u32[]{:S(2)}, u32[]{:S(2)}) collective-permute-start(bf16[128,1024]{1,0:T(8,128)(2,1)} %get-tuple-element.132), channel_id=1, source_target_pairs={{0,12},{4,0},{8,4},{12,8},{1,13},{5,1},{9,5},{13,9},{2,14},{6,2},{... | collective-permute-start | bytes 786440 | tf_op jit(solution)/shard_map/ppermute | solution.py:23
  79.9 16.5 %collective-permute-start.18 = (bf16[128,1024]{1,0:T(8,128)(2,1)}, bf16[128,1024]{1,0:T(8,128)(2,1)S(1)}, u32[]{:S(2)}, u32[]{:S(2)}) collective-permute-start(bf16[128,1024]{1,0:T(8,128)(2,1)} %get-tuple-element.133), channel_id=1, source_target_pairs={{0,8},{4,12},{8,0},{12,4},{1,9},{5,13},{9,1},{13,5},{2,10},{6,14},... | collective-permute-start | bytes 786440 | tf_op jit(solution)/shard_map/ppermute | solution.py:23
  80.5 15.9 %collective-permute-start.19 = (bf16[128,1024]{1,0:T(8,128)(2,1)S(1)}, bf16[128,1024]{1,0:T(8,128)(2,1)S(1)}, u32[]{:S(2)}, u32[]{:S(2)}) collective-permute-start(bf16[128,1024]{1,0:T(8,128)(2,1)S(1)} %copy-done.32), channel_id=1, source_target_pairs={{0,4},{4,8},{8,12},{12,0},{1,5},{5,9},{9,13},{13,1},{2,6},{6,10},{... | collective-permute-start | bytes 786440 | tf_op jit(solution)/shard_map/ppermute | solution.py:23
  85.6 39.0 %all-to-all-start.1 = ((bf16[16,256,256]{2,1,0:T(8,128)(2,1)}), bf16[16,256,256]{2,1,0:T(8,128)(2,1)}, u32[]{:S(2)}, u32[]{:S(2)}) async-start(bf16[16,256,256]{2,1,0:T(8,128)(2,1)} %shard_map.148), calls=%async_computation.1 | async-start | bytes 4194304 | tf_op jit(solution)/shard_map/all_to_all | solution.py:542
  92.5 3.9 %copy-start.20 = (bf16[128,1024]{1,0:T(8,128)(2,1)S(1)}, bf16[128,1024]{1,0:T(8,128)(2,1)}, u32[]{:S(2)}) copy-start(bf16[128,1024]{1,0:T(8,128)(2,1)} %get-tuple-element.131) | copy-start | bytes 786436
  92.5 3.9 %copy-start.30 = (f32[1024]{0:T(1024)S(1)}, f32[1024]{0:T(1024)}, u32[]{:S(2)}) copy-start(f32[1024]{0:T(1024)} %param.16) | copy-start | bytes 12292
  92.5 4.2 %copy-start.3 = (bf16[8,16,1024]{2,1,0:T(8,128)(2,1)S(1)}, bf16[8,16,1024]{2,1,0:T(8,128)(2,1)}, u32[]{:S(2)}) copy-start(bf16[8,16,1024]{2,1,0:T(8,128)(2,1)} %param.19) | copy-start | bytes 786436
  97.0 4.7 %copy-start.4 = (bf16[128,1024]{1,0:T(8,128)(2,1)}, bf16[128,1024]{1,0:T(8,128)(2,1)S(1)}, u32[]{:S(2)}) copy-start(bf16[128,1024]{1,0:T(8,128)(2,1)S(1)} %fusion.8.coarse_grad.right0) | copy-start | bytes 786436
  97.0 11.9 %collective-permute-start.20 = (bf16[128,1024]{1,0:T(8,128)(2,1)S(1)}, bf16[128,1024]{1,0:T(8,128)(2,1)S(1)}, u32[]{:S(2)}, u32[]{:S(2)}) collective-permute-start(bf16[128,1024]{1,0:T(8,128)(2,1)S(1)} %fusion.8.coarse_grad.right0), channel_id=1, source_target_pairs={{0,4},{4,8},{8,12},{12,0},{1,5},{5,9},{9,13},{13,1},{2,6},{6,10},{... | collective-permute-start | bytes 786440 | tf_op jit(solution)/shard_map/ppermute | solution.py:23
  98.3 13.7 %collective-permute-start.21 = (bf16[128,1024]{1,0:T(8,128)(2,1)S(1)}, bf16[128,1024]{1,0:T(8,128)(2,1)S(1)}, u32[]{:S(2)}, u32[]{:S(2)}) collective-permute-start(bf16[128,1024]{1,0:T(8,128)(2,1)S(1)} %fusion.8.coarse_grad.right0), channel_id=1, source_target_pairs={{0,8},{4,12},{8,0},{12,4},{1,9},{5,13},{9,1},{13,5},{2,10},{6,14},... | collective-permute-start | bytes 786440 | tf_op jit(solution)/shard_map/ppermute | solution.py:23
  100.6 11.4 %collective-permute-start.22 = (bf16[128,1024]{1,0:T(8,128)(2,1)S(1)}, bf16[128,1024]{1,0:T(8,128)(2,1)S(1)}, u32[]{:S(2)}, u32[]{:S(2)}) collective-permute-start(bf16[128,1024]{1,0:T(8,128)(2,1)S(1)} %fusion.8.coarse_grad.right0), channel_id=1, source_target_pairs={{0,12},{4,0},{8,4},{12,8},{1,13},{5,1},{9,5},{13,9},{2,14},{6,2},{... | collective-permute-start | bytes 786440 | tf_op jit(solution)/shard_map/ppermute | solution.py:23
  107.8 10.8 %collective-permute-start.24 = (bf16[2,8,16,256]{3,2,1,0:T(8,128)(2,1)}, bf16[2,8,16,256]{3,2,1,0:T(8,128)(2,1)S(1)}, u32[]{:S(2)}, u32[]{:S(2)}) collective-permute-start(bf16[2,8,16,256]{3,2,1,0:T(8,128)(2,1)} %get-tuple-element.152), channel_id=1, source_target_pairs={{0,4},{4,8},{8,12},{12,0},{1,5},{5,9},{9,13},{13,1},{2,6},{6,10},{... | collective-permute-start | bytes 393224 | tf_op jit(solution)/shard_map/ppermute | solution.py:23
  108.1 10.5 %collective-permute-start.25 = (bf16[2,8,16,256]{3,2,1,0:T(8,128)(2,1)}, bf16[2,8,16,256]{3,2,1,0:T(8,128)(2,1)S(1)}, u32[]{:S(2)}, u32[]{:S(2)}) collective-permute-start(bf16[2,8,16,256]{3,2,1,0:T(8,128)(2,1)} %get-tuple-element.153), channel_id=1, source_target_pairs={{0,8},{4,12},{8,0},{12,4},{1,9},{5,13},{9,1},{13,5},{2,10},{6,14},... | collective-permute-start | bytes 393224 | tf_op jit(solution)/shard_map/ppermute | solution.py:23
  109.0 3.0 %copy-start.21 = (bf16[128,1024]{1,0:T(8,128)(2,1)}, bf16[128,1024]{1,0:T(8,128)(2,1)S(1)}, u32[]{:S(2)}) copy-start(bf16[128,1024]{1,0:T(8,128)(2,1)S(1)} %collective-permute-done.20.right1) | copy-start | bytes 786436
  109.0 9.6 %collective-permute-start.26 = (bf16[2,8,16,256]{3,2,1,0:T(8,128)(2,1)}, bf16[2,8,16,256]{3,2,1,0:T(8,128)(2,1)S(1)}, u32[]{:S(2)}, u32[]{:S(2)}) collective-permute-start(bf16[2,8,16,256]{3,2,1,0:T(8,128)(2,1)} %get-tuple-element.154), channel_id=1, source_target_pairs={{0,12},{4,0},{8,4},{12,8},{1,13},{5,1},{9,5},{13,9},{2,14},{6,2},{... | collective-permute-start | bytes 393224 | tf_op jit(solution)/shard_map/ppermute | solution.py:23
  116.0 5.6 %collective-permute-start.23 = (bf16[16,16,1024]{2,1,0:T(8,128)(2,1)}, bf16[16,16,1024]{2,1,0:T(8,128)(2,1)S(1)}, u32[]{:S(2)}, u32[]{:S(2)}) collective-permute-start(bf16[16,16,1024]{2,1,0:T(8,128)(2,1)} %get-tuple-element.150), channel_id=1, source_target_pairs={{0,1},{1,0},{2,3},{3,2},{4,5},{5,4},{6,7},{7,6},{8,9},{9,8},{10,11... | collective-permute-start | bytes 1572872 | tf_op jit(solution)/shard_map/ppermute | solution.py:23
  120.2 1.4 collective-permute-start.27
  124.6 19.1 %all-to-all-start.2 = ((bf16[16,80,256]{2,1,0:T(8,128)(2,1)}), bf16[16,80,256]{2,1,0:T(8,128)(2,1)S(1)}, u32[]{:S(2)}, u32[]{:S(2)}) async-start(bf16[16,80,256]{2,1,0:T(8,128)(2,1)} %shard_map.152), calls=%async_computation.2 | async-start | bytes 1310720 | tf_op jit(solution)/shard_map/all_to_all | solution.py:560
  131.5 23.0 %copy-start.31 = (bf16[128,1024]{1,0:T(8,128)(2,1)S(1)}, bf16[128,1024]{1,0:T(8,128)(2,1)}, u32[]{:S(2)}) copy-start(bf16[128,1024]{1,0:T(8,128)(2,1)} %get-tuple-element.171) | copy-start | bytes 786436
  131.5 37.0 %copy-start.19 = (bf16[128,1024]{1,0:T(8,128)(2,1)S(1)}, bf16[128,1024]{1,0:T(8,128)(2,1)}, u32[]{:S(2)}) copy-start(bf16[128,1024]{1,0:T(8,128)(2,1)} %get-tuple-element.168) | copy-start | bytes 786436
  143.7 0.8 copy-start.2
  146.9 22.5 %all-to-all-start.3 = ((bf16[8,272,256]{2,1,0:T(8,128)(2,1)}), bf16[8,272,256]{2,1,0:T(8,128)(2,1)S(1)}, u32[]{:S(2)}, u32[]{:S(2)}) async-start(bf16[8,272,256]{2,1,0:T(8,128)(2,1)} %get-tuple-element.167), calls=%async_computation.3 | async-start | bytes 2228224 | tf_op jit(solution)/shard_map/all_to_all | solution.py:565
  151.0 7.3 %collective-permute-start.28 = (bf16[128,1024]{1,0:T(8,128)(2,1)}, bf16[128,1024]{1,0:T(8,128)(2,1)S(1)}, u32[]{:S(2)}, u32[]{:S(2)}) collective-permute-start(bf16[128,1024]{1,0:T(8,128)(2,1)} %get-tuple-element.169), channel_id=1, source_target_pairs={{0,12},{4,0},{8,4},{12,8},{1,13},{5,1},{9,5},{13,9},{2,14},{6,2},{... | collective-permute-start | bytes 786440 | tf_op jit(solution)/shard_map/ppermute | solution.py:23
  152.9 8.1 %collective-permute-start.29 = (bf16[128,1024]{1,0:T(8,128)(2,1)}, bf16[128,1024]{1,0:T(8,128)(2,1)S(1)}, u32[]{:S(2)}, u32[]{:S(2)}) collective-permute-start(bf16[128,1024]{1,0:T(8,128)(2,1)} %get-tuple-element.170), channel_id=1, source_target_pairs={{0,8},{4,12},{8,0},{12,4},{1,9},{5,13},{9,1},{13,5},{2,10},{6,14},... | collective-permute-start | bytes 786440 | tf_op jit(solution)/shard_map/ppermute | solution.py:23
  154.4 14.0 %collective-permute-start.30 = (bf16[128,1024]{1,0:T(8,128)(2,1)S(1)}, bf16[128,1024]{1,0:T(8,128)(2,1)S(1)}, u32[]{:S(2)}, u32[]{:S(2)}) collective-permute-start(bf16[128,1024]{1,0:T(8,128)(2,1)S(1)} %copy-done.31), channel_id=1, source_target_pairs={{0,4},{4,8},{8,12},{12,0},{1,5},{5,9},{9,13},{13,1},{2,6},{6,10},{... | collective-permute-start | bytes 786440 | tf_op jit(solution)/shard_map/ppermute | solution.py:23
  169.4 3.1 %copy-start.1 = (bf16[8,272,256]{2,1,0:T(8,128)(2,1)}, bf16[8,272,256]{2,1,0:T(8,128)(2,1)S(1)}, u32[]{:S(2)}) copy-start(bf16[8,272,256]{2,1,0:T(8,128)(2,1)S(1)} %all-to-all-done.3.blocks) | copy-start | bytes 3342340
  169.4 5.8 %collective-permute-start.31 = (bf16[8,16,256]{2,1,0:T(8,128)(2,1)S(1)}, bf16[8,16,256]{2,1,0:T(8,128)(2,1)S(1)}, u32[]{:S(2)}, u32[]{:S(2)}) collective-permute-start(bf16[8,16,256]{2,1,0:T(8,128)(2,1)S(1)} %get-tuple-element.184), channel_id=1, source_target_pairs={{0,4},{4,8},{8,12},{12,0},{1,5},{5,9},{9,13},{13,1},{2,6},{6,10},{... | collective-permute-start | bytes 196616 | tf_op jit(solution)/shard_map/ppermute | solution.py:23
  169.5 5.7 %collective-permute-start.32 = (bf16[8,16,256]{2,1,0:T(8,128)(2,1)S(1)}, bf16[8,16,256]{2,1,0:T(8,128)(2,1)S(1)}, u32[]{:S(2)}, u32[]{:S(2)}) collective-permute-start(bf16[8,16,256]{2,1,0:T(8,128)(2,1)S(1)} %get-tuple-element.184), channel_id=1, source_target_pairs={{0,8},{4,12},{8,0},{12,4},{1,9},{5,13},{9,1},{13,5},{2,10},{6,14},... | collective-permute-start | bytes 196616 | tf_op jit(solution)/shard_map/ppermute | solution.py:23
  170.4 5.1 %collective-permute-start.33 = (bf16[8,16,256]{2,1,0:T(8,128)(2,1)S(1)}, bf16[8,16,256]{2,1,0:T(8,128)(2,1)S(1)}, u32[]{:S(2)}, u32[]{:S(2)}) collective-permute-start(bf16[8,16,256]{2,1,0:T(8,128)(2,1)S(1)} %get-tuple-element.184), channel_id=1, source_target_pairs={{0,12},{4,0},{8,4},{12,8},{1,13},{5,1},{9,5},{13,9},{2,14},{6,2},{... | collective-permute-start | bytes 196616 | tf_op jit(solution)/shard_map/ppermute | solution.py:23
  175.5 2.9 %copy-start.15 = (bf16[4,8,16,256]{3,2,1,0:T(8,128)(2,1)}, bf16[4,8,16,256]{3,2,1,0:T(8,128)(2,1)S(1)}, u32[]{:S(2)}) copy-start(bf16[4,8,16,256]{3,2,1,0:T(8,128)(2,1)S(1)} %pad_maximum_fusion.own) | copy-start | bytes 786436
  175.5 2.9 %collective-permute-start.34 = (bf16[4,8,16,256]{3,2,1,0:T(8,128)(2,1)S(1)}, bf16[4,8,16,256]{3,2,1,0:T(8,128)(2,1)S(1)}, u32[]{:S(2)}, u32[]{:S(2)}) collective-permute-start(bf16[4,8,16,256]{3,2,1,0:T(8,128)(2,1)S(1)} %pad_maximum_fusion.own), channel_id=1, source_target_pairs={{0,1},{1,0},{2,3},{3,2},{4,5},{5,4},{6,7},{7,6},{8,9},{9,8},{10,11... | collective-permute-start | bytes 786440 | tf_op jit(solution)/shard_map/ppermute | solution.py:23
  (8 other events, 5.8 us)
